TPU v7x, 32 devices: a whole 2x2x4 slice. The times are simulated.
32 devices in a mesh: xd: 4 (over z), ta: 8 (over y, x, core).
Axes of the slice: x: 2, y: 2, z: 4, core: 2. Of those that a mesh axis runs over, the one named last changes fastest.
Arguments:
- gauge_links: float32 [4, 2, 3, 3, 16, 8, 4, 128], P(None, None, None, None, 'xd', 'ta'), may hold values from -1 to 1, as said below
- momenta: float32 [4, 2, 3, 3, 16, 8, 4, 128], P(None, None, None, None, 'xd', 'ta'), as said below
- noise_table: float32 [2, 4, 3, 4096], replicated, may hold values from -6 to 6
- noise_index: int32 [16, 8, 4, 128], P('xd', 'ta'), may hold values from 0 to 4095
- partner: int32 [16], P('xd'), may hold values from 0 to 15, as said below
Outputs:
- new_links: float32 [4, 2, 3, 3, 16, 8, 4, 128], P(None, None, None, None, 'xd', 'ta')
- new_momenta: float32 [4, 2, 3, 3, 16, 8, 4, 128], P(None, None, None, None, 'xd', 'ta')
Inputs may be any that keep to these rules, and one draw needn't show every extreme that they name: partner is an involution without fixed points: each row x1 is paired with a row of the aligned block of 4 rows that lies 16 / 2 rows away, and partner[partner[x1]] = x1. Every gauge_links[mu] at every site is a special unitary 3 x 3 matrix. Every momenta[mu] at every site is a Hermitian traceless 3 x 3 matrix.
All inputs are finite; a program needn't handle non-finite values.
Results may differ from a plain program's by a relative error of at most 0.0001.
Values sent between devices are 32-bit elements; how exact they have to be, the bound alone decides.
A program may use at most 128 MiB of HBM per device.

v0:
```python
import jax
import jax.numpy as jnp
from jax import lax
from jax.sharding import PartitionSpec as P

MD_STEPS = 2
DEGREE = 6


hopping = 0.13
step_size = 0.25
gamma_table = (
    ((3, 2, 1, 0), (0, 0, 0, 0), (1, 1, -1, -1)),
    ((2, 3, 0, 1), (1, 1, 1, 1), (0, 0, 0, 0)),
    ((3, 2, 1, 0), (-1, 1, 1, -1), (0, 0, 0, 0)),
    ((2, 3, 0, 1), (0, 0, 0, 0), (1, -1, -1, 1)),
)


def shifted_2(value, axis, by):
    devices = lax.axis_size(axis)
    return lax.ppermute(value, axis, [(i, (i + by) % devices) for i in range(devices)])


def partner_2(value, axis, stride):
    mask = 2**stride
    pairs = [(source, source ^ mask) for source in range(lax.axis_size(axis))]
    return lax.ppermute(value, axis, pairs)


def spin_apply(spinor, direction, sign_factor):
    source_order, real_part, imag_part = gamma_table[direction]
    rows_real = []
    rows_imag = []
    for spin_row in range(4):
        source = source_order[spin_row]
        add_real = spinor[0, source] * (sign_factor * real_part[spin_row]) - spinor[1, source] * (
            sign_factor * imag_part[spin_row]
        )
        add_imag = spinor[1, source] * (sign_factor * real_part[spin_row]) + spinor[0, source] * (
            sign_factor * imag_part[spin_row]
        )
        rows_real.append(spinor[0, spin_row] + add_real)
        rows_imag.append(spinor[1, spin_row] + add_imag)
    return jnp.stack([jnp.stack(rows_real), jnp.stack(rows_imag)])


def mat_vec(matrix, spinor):
    mat_real = matrix[0][None]
    mat_imag = matrix[1][None]
    vec_real = spinor[0][:, None]
    vec_imag = spinor[1][:, None]
    out_real = jnp.sum(mat_real * vec_real - mat_imag * vec_imag, axis=2)
    out_imag = jnp.sum(mat_real * vec_imag + mat_imag * vec_real, axis=2)
    return jnp.stack([out_real, out_imag])


def dagger(matrix):
    return jnp.stack([jnp.swapaxes(matrix[0], 0, 1), -jnp.swapaxes(matrix[1], 0, 1)])


def mat_mat(left_mat, right_mat):
    left_real = left_mat[0][:, :, None]
    left_imag = left_mat[1][:, :, None]
    right_real = right_mat[0][None]
    right_imag = right_mat[1][None]
    return jnp.stack(
        [
            jnp.sum(left_real * right_real - left_imag * right_imag, axis=1),
            jnp.sum(left_real * right_imag + left_imag * right_real, axis=1),
        ]
    )


def outer_sum(first_spin, second_spin):
    first_real = first_spin[0][:, :, None]
    first_imag = first_spin[1][:, :, None]
    second_real = second_spin[0][:, None]
    second_imag = second_spin[1][:, None]
    return jnp.stack(
        [
            jnp.sum(first_real * second_real + first_imag * second_imag, axis=0),
            jnp.sum(first_imag * second_real - first_real * second_imag, axis=0),
        ]
    )


def hermitian_part(matrix):
    swap_real = jnp.swapaxes(matrix[0], 0, 1)
    swap_imag = jnp.swapaxes(matrix[1], 0, 1)
    part_real = (matrix[1] + swap_imag) * 0.5
    part_imag = (swap_real - matrix[0]) * 0.5
    trace_third = (matrix[1][0, 0] + matrix[1][1, 1] + matrix[1][2, 2]) / 3.0
    identity = jnp.eye(3, dtype=jnp.float32).reshape((3, 3) + (1,) * (matrix.ndim - 3))
    return jnp.stack([part_real - identity * trace_third, part_imag])


def link_update(momenta, gauge_links):
    identity = jnp.stack([jnp.eye(3, dtype=jnp.float32), jnp.zeros((3, 3), jnp.float32)]).reshape(
        2, 3, 3, 1, 1, 1, 1
    )
    updated = []
    for direction in range(4):
        generator = jnp.stack(
            [-step_size * momenta[direction, 1], step_size * momenta[direction, 0]]
        )
        series = identity
        for term_index in range(DEGREE, 0, -1):
            series = identity + mat_mat(generator, series) / float(term_index)
        updated.append(mat_mat(series, gauge_links[direction]))
    return jnp.stack(updated)


def move_rows(face_slab, offset):
    return shifted_2(face_slab, "xd", offset)


def move_times(face_slab, offset):
    received = shifted_2(face_slab, "ta", offset)
    boundary = lax.axis_size("ta") - 1 if offset < 0 else 0
    flip_sign = jnp.where(lax.axis_index("ta") == boundary, -1.0, 1.0).astype(face_slab.dtype)
    return received * flip_sign


def move_mirror(face_slab, partner):
    top_bit = lax.axis_size("xd").bit_length() - 2
    received = partner_2(face_slab, "xd", top_bit)
    return jnp.take(received, partner % partner.shape[0], axis=3)


def ahead_of(spinor, partner):
    return [
        jnp.concatenate([spinor[:, :, :, 1:], move_rows(spinor[:, :, :, :1], -1)], axis=3),
        jnp.concatenate([spinor[:, :, :, :, 1:], move_times(spinor, -1)], axis=4),
        jnp.concatenate(
            [spinor[:, :, :, :, :, 1:], move_mirror(spinor[:, :, :, :, :, :1], partner)], axis=5
        ),
        jnp.roll(spinor, -1, axis=6),
    ]


def dirac_dag(gauge_links, spinor, partner):
    behind_all = [mat_vec(dagger(gauge_links[direction]), spinor) for direction in range(4)]
    top_face = behind_all[2][:, :, :, :, :, -1:]
    from_above = move_rows(spinor[:, :, :, :1], -1)
    from_later = move_times(spinor, -1)
    both_faces = move_mirror(
        jnp.concatenate([spinor[:, :, :, :, :, :1], top_face], axis=0), partner
    )
    wrap_face = both_faces[:2]
    wrap_behind = both_faces[2:]
    ahead_all = [
        jnp.concatenate([spinor[:, :, :, 1:], from_above], axis=3),
        jnp.concatenate([spinor[:, :, :, :, 1:], from_later], axis=4),
        jnp.concatenate([spinor[:, :, :, :, :, 1:], wrap_face], axis=5),
        jnp.roll(spinor, -1, axis=6),
    ]
    shifted = [
        jnp.concatenate(
            [move_rows(behind_all[0][:, :, :, -1:], 1), behind_all[0][:, :, :, :-1]], axis=3
        ),
        jnp.concatenate([move_times(behind_all[1], 1), behind_all[1][:, :, :, :, :-1]], axis=4),
        jnp.concatenate([wrap_behind, behind_all[2][:, :, :, :, :, :-1]], axis=5),
        jnp.roll(behind_all[3], 1, axis=6),
    ]
    hop_sum = None
    for direction in range(4):
        ahead = mat_vec(gauge_links[direction], ahead_all[direction])
        hop_term = spin_apply(ahead, direction, 1) + spin_apply(shifted[direction], direction, -1)
        hop_sum = hop_term if direction == 0 else hop_sum + hop_term
    return (spinor - hopping * hop_sum, ahead_all)


def force_term(gauge_links, phi, phi_ahead, response, response_ahead):
    forces = []
    for direction in range(4):
        ahead_field = spin_apply(response_ahead[direction], direction, -1)
        local_field = spin_apply(response, direction, 1)
        bracket = outer_sum(ahead_field, phi) + outer_sum(phi_ahead[direction], local_field)
        forces.append(hermitian_part(mat_mat(gauge_links[direction], bracket)) * (-2.0 * hopping))
    return jnp.stack(forces)


def pack_force(forces):
    real_part = forces[:, 0]
    imag_part = forces[:, 1]
    return jnp.stack(
        [
            real_part[:, 0, 0],
            real_part[:, 1, 1],
            real_part[:, 2, 2],
            real_part[:, 0, 1],
            imag_part[:, 0, 1],
            real_part[:, 0, 2],
            imag_part[:, 0, 2],
            real_part[:, 1, 2],
            imag_part[:, 1, 2],
        ],
        axis=1,
    )


def unpack_force(packed):
    pieces = [packed[:, index] for index in range(9)]
    zeros_part = jnp.zeros_like(pieces[0])
    real_rows = [
        [pieces[0], pieces[3], pieces[5]],
        [pieces[3], pieces[1], pieces[7]],
        [pieces[5], pieces[7], pieces[2]],
    ]
    imag_rows = [
        [zeros_part, pieces[4], pieces[6]],
        [-pieces[4], zeros_part, pieces[8]],
        [-pieces[6], -pieces[8], zeros_part],
    ]
    real_matrix = jnp.stack([jnp.stack(row_list, axis=1) for row_list in real_rows], axis=1)
    imag_matrix = jnp.stack([jnp.stack(row_list, axis=1) for row_list in imag_rows], axis=1)
    return jnp.stack([real_matrix, imag_matrix], axis=1)


def per_device(gauge_links, momenta, noise_table, noise_index, partner):
    noise_field = jnp.take(noise_table, noise_index, axis=3)
    phi, unused = dirac_dag(gauge_links, noise_field, partner)
    top_bit = lax.axis_size("xd").bit_length() - 2
    mirror_rows = partner % partner.shape[0]
    for step_number in range(MD_STEPS):
        response, phi_ahead = dirac_dag(gauge_links, phi, partner)
        response_ahead = ahead_of(response, partner)
        forces = force_term(gauge_links, phi, phi_ahead, response, response_ahead)
        received = partner_2(pack_force(forces), "xd", top_bit)
        mirrored = jnp.take(unpack_force(received), mirror_rows, axis=4)
        total_force = jnp.stack(
            [forces[:, 0] - mirrored[:, 0], forces[:, 1] + mirrored[:, 1]], axis=1
        )
        momenta = momenta + step_size * total_force
        gauge_links = link_update(momenta, gauge_links)
    return (gauge_links, momenta)


def solution(mesh):
    placed = (
        P(None, None, None, None, "xd", "ta", None, None),
        P(None, None, None, None, "xd", "ta", None, None),
        P(),
        P("xd", "ta", None, None),
        P("xd"),
    )
    return jax.shard_map(
        per_device,
        mesh=mesh,
        in_specs=placed,
        out_specs=(
            P(None, None, None, None, "xd", "ta", None, None),
            P(None, None, None, None, "xd", "ta", None, None),
        ),
        check_vma=False,
    )
```

profile of v0, /device:TPU:0, one launch (start us, length us, event | category | flops | bytes accessed | tf_op | source)
XLA Modules:
  0.0 231.2 jit_solution(4502519338205216080)
XLA Ops:
  2.0 14.0 %copy.1747 = f32[2,4,3,4096]{1,0,3,2:T(2,128)} copy(f32[2,4,3,4096]{3,1,2,0:T(4,128)} %param.13) | data formatting | bytes 786432 | tf_op args[2]
  16.0 26.4 %gather_fusion = f32[2048,2,4,3]{2,1,3,0:T(2,128)} fusion(f32[2,4,3,4096]{1,0,3,2:T(2,128)} %copy.1747, s32[2048]{0:T(1024)S(1)} %broadcast_clamp_fusion), kind=kCustom, calls=%fused_computation.7 | custom fusion | bytes 401408 | tf_op jit(solution)/shard_map/jit(_take)/gather | solution.py:222
  42.4 7.8 %copy.1748 = f32[4,4,128,2,4,3]{2,0,5,1,4,3:T(4,128)S(1)} copy(f32[4,4,128,2,4,3]{4,3,5,2,1,0:T(2,128)} %bitcast.4389) | data formatting | bytes 393216 | tf_op jit(solution)/shard_map/jit(_take)/gather | solution.py:222
  50.3 3.4 %collective-permute-start.2 = (f32[2,4,3,4,1,4,128]{6,3,2,5,4,1,0:T(4,128)S(1)}, f32[2,4,3,4,1,4,128]{6,3,2,5,4,1,0:T(4,128)S(1)}, u32[]{:S(2)}, u32[]{:S(2)}) collective-permute-start(f32[2,4,3,4,1,4,128]{6,3,2,5,4,1,0:T(4,128)S(1)} %bitcast_select_fusion.1), channel_id=1, source_target_pairs={{0,7},{1,0},{2,1},{3,2},{4,3},{5,4},{6,5},{7,6},{8,15},{9,8},{10,9... | collective-permute-start | bytes 589832 | tf_op jit(solution)/shard_map/ppermute | solution.py:22
  54.1 1.3 subtract_reduce_fusion.32
  56.2 1.6 collective-permute-start.1
  58.0 2.6 %collective-permute-start.4 = (f32[4,4,3,4,1,1,128]{6,1,3,2,0,5,4:T(4,128)S(1)}, f32[4,4,3,4,1,1,128]{6,1,3,2,0,5,4:T(4,128)S(1)}, u32[]{:S(2)}, u32[]{:S(2)}) collective-permute-start(f32[4,4,3,4,1,1,128]{6,1,3,2,0,5,4:T(4,128)S(1)} %fusion.94), channel_id=1, source_target_pairs={{0,16},{8,24},{16,0},{24,8},{1,17},{9,25},{17,1},{25,9},{2,18},{10... | collective-permute-start | bytes 294920 | tf_op jit(solution)/shard_map/ppermute | solution.py:28
  61.4 1.4 collective-permute-start
  69.0 1.0 broadcast_multiply_fusion.2
  71.1 2.6 %subtract_reduce_fusion.24 = (f32[4,3,4,4,128]{4,3,2,1,0:T(4,128)S(1)}, f32[4,3,4,4,128]{4,3,2,1,0:T(4,128)S(1)}, f32[4,3,4,4,128]{4,3,2,1,0:T(4,128)S(1)}, f32[...) fusion(f32[4,3,4,4,128]{4,3,2,1,0:T(4,128)S(1)} %copy.1915, ...), kind=kLoop, calls=%fused_computation.110 | loop fusion | flops 2162688 | bytes 1572864 | tf_op jit(solution)/shard_map/reduce_sum | solution.py:53
  74.2 1.0 fusion.414
  76.3 2.1 collective-permute-start.7
  78.8 3.0 %collective-permute-start.6 = (f32[2,4,3,1,1,4,128]{6,3,2,5,4,1,0:T(1,128)S(1)}, f32[2,4,3,1,1,4,128]{6,3,2,5,4,1,0:T(1,128)S(1)}, u32[]{:S(2)}, u32[]{:S(2)}) collective-permute-start(f32[2,4,3,1,1,4,128]{6,3,2,5,4,1,0:T(1,128)S(1)} %pad_maximum_fusion.27), channel_id=1, source_target_pairs={{0,8},{8,16},{16,24},{24,0},{1,9},{9,17},{17,25},{25,1},{2,10},{10... | collective-permute-start | bytes 147464 | tf_op jit(solution)/shard_map/ppermute | solution.py:22
  84.3 13.7 %collective-permute-start.5 = (f32[2,4,3,1,1,4,128]{6,3,2,5,1,4,0:T(1,128)S(1)}, f32[2,4,3,1,1,4,128]{6,3,2,5,1,4,0:T(1,128)S(1)}, u32[]{:S(2)}, u32[]{:S(2)}) collective-permute-start(f32[2,4,3,1,1,4,128]{6,3,2,5,1,4,0:T(1,128)S(1)} %slice.3143), channel_id=1, source_target_pairs={{0,24},{8,0},{16,8},{24,16},{1,25},{9,1},{17,9},{25,17},{2,26},{10... | collective-permute-start | bytes 147464 | tf_op jit(solution)/shard_map/ppermute | solution.py:22
  98.2 3.0 %collective-permute-done.5 = f32[2,4,3,1,1,4,128]{6,3,2,5,1,4,0:T(1,128)S(1)} collective-permute-done((f32[2,4,3,1,1,4,128]{6,3,2,5,1,4,0:T(1,128)S(1)}, f32[2,4,3,1,1,4,128]{6,3,2,5,1,4,0:T(1,128)S(1)}, u32[]{:S(2)}, u32[]{:S(2)}) %collective-permute-start.5) | collective-permute-done | bytes 49184 | tf_op jit(solution)/shard_map/ppermute | solution.py:22
  104.8 1.0 broadcast_multiply_fusion.1
  105.9 1.0 broadcast_multiply_fusion.5
  116.0 2.6 %collective-permute-start.10 = (f32[2,4,3,1,1,4,128]{6,3,2,5,4,1,0:T(1,128)}, f32[2,4,3,1,1,4,128]{6,3,2,5,4,1,0:T(1,128)}, u32[]{:S(2)}, u32[]{:S(2)}) collective-permute-start(f32[2,4,3,1,1,4,128]{6,3,2,5,4,1,0:T(1,128)} %slice.3227), channel_id=1, source_target_pairs={{0,24},{8,0},{16,8},{24,16},{1,25},{9,1},{17,9},{25,17},{2,26},{10... | collective-permute-start | bytes 147464 | tf_op jit(solution)/shard_map/ppermute | solution.py:22
  119.6 1.7 collective-permute-done.10
  121.3 1.0 bitcast_add_fusion.90
  122.2 0.9 fusion.293
  123.3 1.0 broadcast_multiply_fusion.4
  124.5 0.9 add_reduce_fusion.23
  125.4 1.0 maximum_add_fusion.14
  126.7 1.0 maximum_add_fusion.13
  130.2 1.8 collective-permute-start.13
  132.1 13.1 %collective-permute-done.13 = f32[4,9,4,1,4,128]{5,4,2,0,3,1:T(4,128)S(1)} collective-permute-done((f32[4,9,4,1,4,128]{5,4,2,0,3,1:T(4,128)S(1)}, f32[4,9,4,1,4,128]{5,4,2,0,3,1:T(4,128)S(1)}, u32[]{:S(2)}, u32[]{:S(2)}) %collective-permute-start.13) | collective-permute-done | bytes 294944 | tf_op jit(solution)/shard_map/ppermute | solution.py:28
  146.4 1.9 gather_fusion.4
  148.2 1.3 copy_select_fusion
  149.5 1.1 slice_subtract_fusion.1
  161.3 1.4 subtract_reduce_fusion.8
  164.3 2.9 %collective-permute-start.16 = (f32[4,4,3,4,1,1,128]{6,3,2,5,4,1,0:T(4,128)S(1)}, f32[4,4,3,4,1,1,128]{6,3,2,5,4,1,0:T(4,128)S(1)}, u32[]{:S(2)}, u32[]{:S(2)}) collective-permute-start(f32[4,4,3,4,1,1,128]{6,3,2,5,4,1,0:T(4,128)S(1)} %pad_maximum_fusion.14), channel_id=1, source_target_pairs={{0,16},{8,24},{16,0},{24,8},{1,17},{9,25},{17,1},{25,9},{2,18},{10... | collective-permute-start | bytes 294920 | tf_op jit(solution)/shard_map/ppermute | solution.py:28
  174.7 2.3 gather_fusion.5
  177.1 1.1 bitcast_select_fusion.2
  178.2 1.0 fusion.75
  179.2 1.2 subtract_reduce_fusion.10
  180.5 1.0 fusion.3
  181.8 1.0 broadcast_multiply_fusion
  182.9 2.0 fusion.413
  190.9 2.4 %collective-permute-start.18 = (f32[2,4,3,4,1,4,128]{6,3,2,5,4,1,0:T(4,128)S(1)}, f32[2,4,3,4,1,4,128]{6,3,2,5,4,1,0:T(4,128)S(1)}, u32[]{:S(2)}, u32[]{:S(2)}) collective-permute-start(f32[2,4,3,4,1,4,128]{6,3,2,5,4,1,0:T(4,128)S(1)} %fusion.413), channel_id=1, source_target_pairs={{0,7},{1,0},{2,1},{3,2},{4,3},{5,4},{6,5},{7,6},{8,15},{9,8},{10,9... | collective-permute-start | bytes 589832 | tf_op jit(solution)/shard_map/ppermute | solution.py:22
  193.4 3.8 %collective-permute-start.17 = (f32[2,4,3,1,1,4,128]{6,3,2,5,4,1,0:T(1,128)S(1)}, f32[2,4,3,1,1,4,128]{6,3,2,5,4,1,0:T(1,128)S(1)}, u32[]{:S(2)}, u32[]{:S(2)}) collective-permute-start(f32[2,4,3,1,1,4,128]{6,3,2,5,4,1,0:T(1,128)S(1)} %slice.3459), channel_id=1, source_target_pairs={{0,24},{8,0},{16,8},{24,16},{1,25},{9,1},{17,9},{25,17},{2,26},{10... | collective-permute-start | bytes 147464 | tf_op jit(solution)/shard_map/ppermute | solution.py:22
  200.5 1.0 maximum_add_fusion.22
  201.7 1.0 maximum_add_fusion.21
  204.5 1.5 collective-permute-start.20
  206.0 12.3 %collective-permute-done.20 = f32[4,9,4,1,4,128]{5,4,0,2,3,1:T(4,128)S(1)} collective-permute-done((f32[4,9,4,1,4,128]{5,4,0,2,3,1:T(4,128)S(1)}, f32[4,9,4,1,4,128]{5,4,0,2,3,1:T(4,128)S(1)}, u32[]{:S(2)}, u32[]{:S(2)}) %collective-permute-start.20) | collective-permute-done | bytes 294944 | tf_op jit(solution)/shard_map/ppermute | solution.py:28
  218.8 1.1 gather_fusion.7
  220.3 1.1 fusion.412
  230.0 0.9 maximum_bitcast_fusion.2
  (822 shorter events, 70.3 us)
Async XLA Ops:
  2.0 51.7 %copy-start.78 = (f32[4,2,3,3,4,1,4,128]{7,6,5,4,3,2,1,0:T(4,128)S(1)}, f32[4,2,3,3,4,1,4,128]{7,6,5,4,3,2,1,0:T(4,128)}, u32[]{:S(2)}) copy-start(f32[4,2,3,3,4,1,4,128]{7,6,5,4,3,2,1,0:T(4,128)} %param.11) | copy-start | bytes 1769476
  42.4 21.7 %copy-start.96 = (s32[4]{0:T(128)S(1)}, s32[4]{0:T(128)}, u32[]{:S(2)}) copy-start(s32[4]{0:T(128)} %param.15) | copy-start | bytes 52
  50.3 19.8 %collective-permute-start.2 = (f32[2,4,3,4,1,4,128]{6,3,2,5,4,1,0:T(4,128)S(1)}, f32[2,4,3,4,1,4,128]{6,3,2,5,4,1,0:T(4,128)S(1)}, u32[]{:S(2)}, u32[]{:S(2)}) collective-permute-start(f32[2,4,3,4,1,4,128]{6,3,2,5,4,1,0:T(4,128)S(1)} %bitcast_select_fusion.1), channel_id=1, source_target_pairs={{0,7},{1,0},{2,1},{3,2},{4,3},{5,4},{6,5},{7,6},{8,15},{9,8},{10,9... | collective-permute-start | bytes 589832 | tf_op jit(solution)/shard_map/ppermute | solution.py:22
  54.0 72.4 %copy-start.19 = (f32[3,3,4,4,128]{4,3,2,1,0:T(4,128)}, f32[3,3,4,4,128]{4,3,2,1,0:T(4,128)S(1)}, u32[]{:S(2)}) copy-start(f32[3,3,4,4,128]{4,3,2,1,0:T(4,128)S(1)} %get-tuple-element.309) | copy-start | bytes 221188
  54.0 72.4 %copy-start.21 = (f32[3,3,4,4,128]{4,3,2,1,0:T(4,128)}, f32[3,3,4,4,128]{4,3,2,1,0:T(4,128)S(1)}, u32[]{:S(2)}) copy-start(f32[3,3,4,4,128]{4,3,2,1,0:T(4,128)S(1)} %get-tuple-element.313) | copy-start | bytes 221188
  54.0 73.7 %copy-start.27 = (f32[3,3,4,4,128]{4,3,2,1,0:T(4,128)}, f32[3,3,4,4,128]{4,3,2,1,0:T(4,128)S(1)}, u32[]{:S(2)}) copy-start(f32[3,3,4,4,128]{4,3,2,1,0:T(4,128)S(1)} %get-tuple-element.314) | copy-start | bytes 221188
  54.0 73.7 %copy-start.29 = (f32[3,3,4,4,128]{4,3,2,1,0:T(4,128)}, f32[3,3,4,4,128]{4,3,2,1,0:T(4,128)S(1)}, u32[]{:S(2)}) copy-start(f32[3,3,4,4,128]{4,3,2,1,0:T(4,128)S(1)} %get-tuple-element.315) | copy-start | bytes 221188
  54.0 74.0 %copy-start.31 = (f32[3,3,4,4,128]{4,3,2,1,0:T(4,128)}, f32[3,3,4,4,128]{4,3,2,1,0:T(4,128)S(1)}, u32[]{:S(2)}) copy-start(f32[3,3,4,4,128]{4,3,2,1,0:T(4,128)S(1)} %get-tuple-element.316) | copy-start | bytes 221188
  54.1 74.0 %copy-start.33 = (f32[3,3,4,4,128]{4,3,2,1,0:T(4,128)}, f32[3,3,4,4,128]{4,3,2,1,0:T(4,128)S(1)}, u32[]{:S(2)}) copy-start(f32[3,3,4,4,128]{4,3,2,1,0:T(4,128)S(1)} %get-tuple-element.317) | copy-start | bytes 221188
  54.1 74.3 %copy-start.23 = (f32[3,3,4,4,128]{4,3,2,1,0:T(4,128)}, f32[3,3,4,4,128]{4,3,2,1,0:T(4,128)S(1)}, u32[]{:S(2)}) copy-start(f32[3,3,4,4,128]{4,3,2,1,0:T(4,128)S(1)} %get-tuple-element.303) | copy-start | bytes 221188
  54.1 74.3 %copy-start.25 = (f32[3,3,4,4,128]{4,3,2,1,0:T(4,128)}, f32[3,3,4,4,128]{4,3,2,1,0:T(4,128)S(1)}, u32[]{:S(2)}) copy-start(f32[3,3,4,4,128]{4,3,2,1,0:T(4,128)S(1)} %get-tuple-element.318) | copy-start | bytes 221188
  56.2 8.2 %collective-permute-start.1 = (f32[2,4,3,1,1,4,128]{6,3,2,5,4,1,0:T(1,128)}, f32[2,4,3,1,1,4,128]{6,3,2,5,4,1,0:T(1,128)}, u32[]{:S(2)}, u32[]{:S(2)}) collective-permute-start(f32[2,4,3,1,1,4,128]{6,3,2,5,4,1,0:T(1,128)} %pad_maximum_fusion.28), channel_id=1, source_target_pairs={{0,8},{8,16},{16,24},{24,0},{1,9},{9,17},{17,25},{25,1},{2,10},{10... | collective-permute-start | bytes 147464 | tf_op jit(solution)/shard_map/ppermute | solution.py:22
  58.0 9.3 %collective-permute-start.4 = (f32[4,4,3,4,1,1,128]{6,1,3,2,0,5,4:T(4,128)S(1)}, f32[4,4,3,4,1,1,128]{6,1,3,2,0,5,4:T(4,128)S(1)}, u32[]{:S(2)}, u32[]{:S(2)}) collective-permute-start(f32[4,4,3,4,1,1,128]{6,1,3,2,0,5,4:T(4,128)S(1)} %fusion.94), channel_id=1, source_target_pairs={{0,16},{8,24},{16,0},{24,8},{1,17},{9,25},{17,1},{25,9},{2,18},{10... | collective-permute-start | bytes 294920 | tf_op jit(solution)/shard_map/ppermute | solution.py:28
  60.7 8.3 %collective-permute-start.3 = (f32[2,4,3,4,1,4,128]{6,3,2,5,4,1,0:T(4,128)S(1)}, f32[2,4,3,4,1,4,128]{6,3,2,5,4,1,0:T(4,128)}, u32[]{:S(2)}, u32[]{:S(2)}) collective-permute-start(f32[2,4,3,4,1,4,128]{6,3,2,5,4,1,0:T(4,128)S(1)} %pad_maximum_fusion.11), channel_id=1, source_target_pairs={{0,1},{1,2},{2,3},{3,4},{4,5},{5,6},{6,7},{7,0},{8,9},{9,10},{10,1... | collective-permute-start | bytes 589832 | tf_op jit(solution)/shard_map/ppermute | solution.py:22
  61.4 4.4 %collective-permute-start = (f32[2,4,3,1,1,4,128]{6,3,2,5,4,1,0:T(1,128)}, f32[2,4,3,1,1,4,128]{6,3,2,5,4,1,0:T(1,128)}, u32[]{:S(2)}, u32[]{:S(2)}) collective-permute-start(f32[2,4,3,1,1,4,128]{6,3,2,5,4,1,0:T(1,128)} %slice.3059), channel_id=1, source_target_pairs={{0,24},{8,0},{16,8},{24,16},{1,25},{9,1},{17,9},{25,17},{2,26},{10... | collective-permute-start | bytes 147464 | tf_op jit(solution)/shard_map/ppermute | solution.py:22
  64.1 54.5 %copy-start.95 = (s32[1024]{0:T(1024)}, s32[1024]{0:T(1024)S(1)}, u32[]{:S(2)}) copy-start(s32[1024]{0:T(1024)S(1)} %pad_clamp_fusion) | copy-start | bytes 12292
  71.1 53.4 %copy-start.1 = (f32[4,3,4,4,128]{4,3,2,1,0:T(4,128)}, f32[4,3,4,4,128]{4,3,2,1,0:T(4,128)S(1)}, u32[]{:S(2)}) copy-start(f32[4,3,4,4,128]{4,3,2,1,0:T(4,128)S(1)} %copy.1915) | copy-start | bytes 294916
  75.2 32.3 %copy-start.59 = (f32[2,4,3,4,1,3,128]{6,3,2,5,1,4,0:T(4,128)}, f32[2,4,3,4,1,3,128]{6,3,2,5,1,4,0:T(4,128)S(1)}, u32[]{:S(2)}) copy-start(f32[2,4,3,4,1,3,128]{6,3,2,5,1,4,0:T(4,128)S(1)} %slice.3182) | copy-start | bytes 442372
  76.3 31.4 %copy-start.79 = (f32[2,4,3,4,1,1,128]{6,3,2,5,4,1,0:T(4,128)}, f32[2,4,3,4,1,1,128]{6,3,2,5,4,1,0:T(4,128)S(1)}, u32[]{:S(2)}) copy-start(f32[2,4,3,4,1,1,128]{6,3,2,5,4,1,0:T(4,128)S(1)} %slice.3183) | copy-start | bytes 147460
  76.3 29.6 %collective-permute-start.7 = (f32[2,4,3,4,1,4,128]{6,3,2,5,4,1,0:T(4,128)}, f32[2,4,3,4,1,4,128]{6,3,2,5,4,1,0:T(4,128)}, u32[]{:S(2)}, u32[]{:S(2)}) collective-permute-start(f32[2,4,3,4,1,4,128]{6,3,2,5,4,1,0:T(4,128)} %fusion.414), channel_id=1, source_target_pairs={{0,7},{1,0},{2,1},{3,2},{4,3},{5,4},{6,5},{7,6},{8,15},{9,8},{10,9... | collective-permute-start | bytes 589832 | tf_op jit(solution)/shard_map/ppermute | solution.py:22
  78.5 24.2 %collective-permute-start.9 = (f32[4,4,3,4,1,1,128]{6,3,2,5,4,1,0:T(4,128)S(1)}, f32[4,4,3,4,1,1,128]{6,3,2,5,4,1,0:T(4,128)S(1)}, u32[]{:S(2)}, u32[]{:S(2)}) collective-permute-start(f32[4,4,3,4,1,1,128]{6,3,2,5,4,1,0:T(4,128)S(1)} %pad_maximum_fusion.15), channel_id=1, source_target_pairs={{0,16},{8,24},{16,0},{24,8},{1,17},{9,25},{17,1},{25,9},{2,18},{10... | collective-permute-start | bytes 294920 | tf_op jit(solution)/shard_map/ppermute | solution.py:28
  78.8 19.2 %collective-permute-start.6 = (f32[2,4,3,1,1,4,128]{6,3,2,5,4,1,0:T(1,128)S(1)}, f32[2,4,3,1,1,4,128]{6,3,2,5,4,1,0:T(1,128)S(1)}, u32[]{:S(2)}, u32[]{:S(2)}) collective-permute-start(f32[2,4,3,1,1,4,128]{6,3,2,5,4,1,0:T(1,128)S(1)} %pad_maximum_fusion.27), channel_id=1, source_target_pairs={{0,8},{8,16},{16,24},{24,0},{1,9},{9,17},{17,25},{25,1},{2,10},{10... | collective-permute-start | bytes 147464 | tf_op jit(solution)/shard_map/ppermute | solution.py:22
  84.2 29.2 %copy-start.3 = (f32[4,3,4,4,128]{4,3,2,1,0:T(4,128)}, f32[4,3,4,4,128]{4,3,2,1,0:T(4,128)S(1)}, u32[]{:S(2)}) copy-start(f32[4,3,4,4,128]{4,3,2,1,0:T(4,128)S(1)} %copy.2010) | copy-start | bytes 294916
  84.2 29.2 %copy-start.5 = (f32[4,3,4,4,128]{4,3,2,1,0:T(4,128)}, f32[4,3,4,4,128]{4,3,2,1,0:T(4,128)S(1)}, u32[]{:S(2)}) copy-start(f32[4,3,4,4,128]{4,3,2,1,0:T(4,128)S(1)} %copy.2011) | copy-start | bytes 294916
  84.2 20.6 %collective-permute-start.8 = (f32[2,4,3,4,1,4,128]{6,3,2,5,4,1,0:T(4,128)}, f32[2,4,3,4,1,4,128]{6,3,2,5,4,1,0:T(4,128)}, u32[]{:S(2)}, u32[]{:S(2)}) collective-permute-start(f32[2,4,3,4,1,4,128]{6,3,2,5,4,1,0:T(4,128)} %pad_maximum_fusion.12), channel_id=1, source_target_pairs={{0,1},{1,2},{2,3},{3,4},{4,5},{5,6},{6,7},{7,0},{8,9},{9,10},{10,1... | collective-permute-start | bytes 589832 | tf_op jit(solution)/shard_map/ppermute | solution.py:22
  84.3 16.9 %collective-permute-start.5 = (f32[2,4,3,1,1,4,128]{6,3,2,5,1,4,0:T(1,128)S(1)}, f32[2,4,3,1,1,4,128]{6,3,2,5,1,4,0:T(1,128)S(1)}, u32[]{:S(2)}, u32[]{:S(2)}) collective-permute-start(f32[2,4,3,1,1,4,128]{6,3,2,5,1,4,0:T(1,128)S(1)} %slice.3143), channel_id=1, source_target_pairs={{0,24},{8,0},{16,8},{24,16},{1,25},{9,1},{17,9},{25,17},{2,26},{10... | collective-permute-start | bytes 147464 | tf_op jit(solution)/shard_map/ppermute | solution.py:22
  109.8 8.8 %collective-permute-start.12 = (f32[2,4,3,4,1,1,128]{6,3,2,5,4,1,0:T(4,128)S(1)}, f32[2,4,3,4,1,1,128]{6,3,2,5,4,1,0:T(4,128)S(1)}, u32[]{:S(2)}, u32[]{:S(2)}) collective-permute-start(f32[2,4,3,4,1,1,128]{6,3,2,5,4,1,0:T(4,128)S(1)} %slice.3269), channel_id=1, source_target_pairs={{0,16},{8,24},{16,0},{24,8},{1,17},{9,25},{17,1},{25,9},{2,18},{10... | collective-permute-start | bytes 147464 | tf_op jit(solution)/shard_map/ppermute | solution.py:28
  114.4 8.9 %collective-permute-start.11 = (f32[2,4,3,4,1,4,128]{6,3,2,5,4,1,0:T(4,128)S(1)}, f32[2,4,3,4,1,4,128]{6,3,2,5,4,1,0:T(4,128)}, u32[]{:S(2)}, u32[]{:S(2)}) collective-permute-start(f32[2,4,3,4,1,4,128]{6,3,2,5,4,1,0:T(4,128)S(1)} %fusion.21), channel_id=1, source_target_pairs={{0,7},{1,0},{2,1},{3,2},{4,3},{5,4},{6,5},{7,6},{8,15},{9,8},{10,9... | collective-permute-start | bytes 589832 | tf_op jit(solution)/shard_map/ppermute | solution.py:22
  116.0 5.2 %collective-permute-start.10 = (f32[2,4,3,1,1,4,128]{6,3,2,5,4,1,0:T(1,128)}, f32[2,4,3,1,1,4,128]{6,3,2,5,4,1,0:T(1,128)}, u32[]{:S(2)}, u32[]{:S(2)}) collective-permute-start(f32[2,4,3,1,1,4,128]{6,3,2,5,4,1,0:T(1,128)} %slice.3227), channel_id=1, source_target_pairs={{0,24},{8,0},{16,8},{24,16},{1,25},{9,1},{17,9},{25,17},{2,26},{10... | collective-permute-start | bytes 147464 | tf_op jit(solution)/shard_map/ppermute | solution.py:22
  128.0 22.6 %copy-start = (f32[4,2,3,3,4,1,4,128]{7,6,5,4,3,2,1,0:T(4,128)S(1)}, f32[4,2,3,3,4,1,4,128]{7,6,5,4,3,2,1,0:T(4,128)}, u32[]{:S(2)}) copy-start(f32[4,2,3,3,4,1,4,128]{7,6,5,4,3,2,1,0:T(4,128)} %param.12) | copy-start | bytes 1769476
  130.2 15.0 %collective-permute-start.13 = (f32[4,9,4,1,4,128]{5,4,2,0,3,1:T(4,128)S(1)}, f32[4,9,4,1,4,128]{5,4,2,0,3,1:T(4,128)S(1)}, u32[]{:S(2)}, u32[]{:S(2)}) collective-permute-start(f32[4,9,4,1,4,128]{5,4,2,0,3,1:T(4,128)S(1)} %constant_dynamic-update-slice_fusion), channel_id=1, source_target_pairs={{0,16},{8,24},{16,0},{24,8},{1,17},{9,25},{17,1},{25,9},{2,18},{10... | collective-permute-start | bytes 884744 | tf_op jit(solution)/shard_map/ppermute | solution.py:28
  160.0 22.9 %copy-start.41 = (f32[3,3,4,4,128]{4,3,2,1,0:T(4,128)}, f32[3,3,4,4,128]{4,3,2,1,0:T(4,128)S(1)}, u32[]{:S(2)}) copy-start(f32[3,3,4,4,128]{4,3,2,1,0:T(4,128)S(1)} %get-tuple-element.145) | copy-start | bytes 221188
  160.7 22.2 %copy-start.44 = (f32[3,3,4,4,128]{4,3,2,1,0:T(4,128)}, f32[3,3,4,4,128]{4,3,2,1,0:T(4,128)S(1)}, u32[]{:S(2)}) copy-start(f32[3,3,4,4,128]{4,3,2,1,0:T(4,128)S(1)} %get-tuple-element.147) | copy-start | bytes 221188
  163.3 9.3 %collective-permute-start.14 = (f32[2,4,3,1,1,4,128]{6,3,2,5,4,1,0:T(1,128)S(1)}, f32[2,4,3,1,1,4,128]{6,3,2,5,4,1,0:T(1,128)S(1)}, u32[]{:S(2)}, u32[]{:S(2)}) collective-permute-start(f32[2,4,3,1,1,4,128]{6,3,2,5,4,1,0:T(1,128)S(1)} %pad_maximum_fusion.26), channel_id=1, source_target_pairs={{0,8},{8,16},{16,24},{24,0},{1,9},{9,17},{17,25},{25,1},{2,10},{10... | collective-permute-start | bytes 147464 | tf_op jit(solution)/shard_map/ppermute | solution.py:22
  164.2 17.6 %collective-permute-start.15 = (f32[2,4,3,4,1,4,128]{6,3,2,5,4,1,0:T(4,128)}, f32[2,4,3,4,1,4,128]{6,3,2,5,4,1,0:T(4,128)}, u32[]{:S(2)}, u32[]{:S(2)}) collective-permute-start(f32[2,4,3,4,1,4,128]{6,3,2,5,4,1,0:T(4,128)} %pad_maximum_fusion.13), channel_id=1, source_target_pairs={{0,1},{1,2},{2,3},{3,4},{4,5},{5,6},{6,7},{7,0},{8,9},{9,10},{10,1... | collective-permute-start | bytes 589832 | tf_op jit(solution)/shard_map/ppermute | solution.py:22
  164.3 9.8 %collective-permute-start.16 = (f32[4,4,3,4,1,1,128]{6,3,2,5,4,1,0:T(4,128)S(1)}, f32[4,4,3,4,1,1,128]{6,3,2,5,4,1,0:T(4,128)S(1)}, u32[]{:S(2)}, u32[]{:S(2)}) collective-permute-start(f32[4,4,3,4,1,1,128]{6,3,2,5,4,1,0:T(4,128)S(1)} %pad_maximum_fusion.14), channel_id=1, source_target_pairs={{0,16},{8,24},{16,0},{24,8},{1,17},{9,25},{17,1},{25,9},{2,18},{10... | collective-permute-start | bytes 294920 | tf_op jit(solution)/shard_map/ppermute | solution.py:28
  185.9 15.6 %copy-start.45 = (f32[3,3,4,4,128]{4,3,2,1,0:T(4,128)S(1)}, f32[3,3,4,4,128]{4,3,2,1,0:T(4,128)}, u32[]{:S(2)}) copy-start(f32[3,3,4,4,128]{4,3,2,1,0:T(4,128)} %copy-done.44) | copy-start | bytes 221188
  186.4 16.3 %copy-start.39 = (f32[3,3,4,4,128]{4,3,2,1,0:T(4,128)S(1)}, f32[3,3,4,4,128]{4,3,2,1,0:T(4,128)}, u32[]{:S(2)}) copy-start(f32[3,3,4,4,128]{4,3,2,1,0:T(4,128)} %copy-done.38) | copy-start | bytes 221188
  186.4 16.3 %copy-start.51 = (f32[3,3,4,4,128]{4,3,2,1,0:T(4,128)S(1)}, f32[3,3,4,4,128]{4,3,2,1,0:T(4,128)}, u32[]{:S(2)}) copy-start(f32[3,3,4,4,128]{4,3,2,1,0:T(4,128)} %copy-done.50) | copy-start | bytes 221188
  186.6 16.5 %copy-start.36 = (f32[3,3,4,4,128]{4,3,2,1,0:T(4,128)S(1)}, f32[3,3,4,4,128]{4,3,2,1,0:T(4,128)}, u32[]{:S(2)}) copy-start(f32[3,3,4,4,128]{4,3,2,1,0:T(4,128)} %copy-done.35) | copy-start | bytes 221188
  186.6 16.5 %copy-start.48 = (f32[3,3,4,4,128]{4,3,2,1,0:T(4,128)S(1)}, f32[3,3,4,4,128]{4,3,2,1,0:T(4,128)}, u32[]{:S(2)}) copy-start(f32[3,3,4,4,128]{4,3,2,1,0:T(4,128)} %copy-done.47) | copy-start | bytes 221188
  186.7 10.5 %collective-permute-start.19 = (f32[2,4,3,4,1,1,128]{6,3,2,5,1,4,0:T(4,128)S(1)}, f32[2,4,3,4,1,1,128]{6,3,2,5,1,4,0:T(4,128)S(1)}, u32[]{:S(2)}, u32[]{:S(2)}) collective-permute-start(f32[2,4,3,4,1,1,128]{6,3,2,5,1,4,0:T(4,128)S(1)} %slice.3501), channel_id=1, source_target_pairs={{0,16},{8,24},{16,0},{24,8},{1,17},{9,25},{17,1},{25,9},{2,18},{10... | collective-permute-start | bytes 147464 | tf_op jit(solution)/shard_map/ppermute | solution.py:28
  187.0 16.4 %copy-start.42 = (f32[3,3,4,4,128]{4,3,2,1,0:T(4,128)S(1)}, f32[3,3,4,4,128]{4,3,2,1,0:T(4,128)}, u32[]{:S(2)}) copy-start(f32[3,3,4,4,128]{4,3,2,1,0:T(4,128)} %copy-done.41) | copy-start | bytes 221188
  187.0 16.4 %copy-start.54 = (f32[3,3,4,4,128]{4,3,2,1,0:T(4,128)S(1)}, f32[3,3,4,4,128]{4,3,2,1,0:T(4,128)}, u32[]{:S(2)}) copy-start(f32[3,3,4,4,128]{4,3,2,1,0:T(4,128)} %copy-done.53) | copy-start | bytes 221188
  190.9 8.4 %collective-permute-start.18 = (f32[2,4,3,4,1,4,128]{6,3,2,5,4,1,0:T(4,128)S(1)}, f32[2,4,3,4,1,4,128]{6,3,2,5,4,1,0:T(4,128)S(1)}, u32[]{:S(2)}, u32[]{:S(2)}) collective-permute-start(f32[2,4,3,4,1,4,128]{6,3,2,5,4,1,0:T(4,128)S(1)} %fusion.413), channel_id=1, source_target_pairs={{0,7},{1,0},{2,1},{3,2},{4,3},{5,4},{6,5},{7,6},{8,15},{9,8},{10,9... | collective-permute-start | bytes 589832 | tf_op jit(solution)/shard_map/ppermute | solution.py:22
  193.4 5.5 %collective-permute-start.17 = (f32[2,4,3,1,1,4,128]{6,3,2,5,4,1,0:T(1,128)S(1)}, f32[2,4,3,1,1,4,128]{6,3,2,5,4,1,0:T(1,128)S(1)}, u32[]{:S(2)}, u32[]{:S(2)}) collective-permute-start(f32[2,4,3,1,1,4,128]{6,3,2,5,4,1,0:T(1,128)S(1)} %slice.3459), channel_id=1, source_target_pairs={{0,24},{8,0},{16,8},{24,16},{1,25},{9,1},{17,9},{25,17},{2,26},{10... | collective-permute-start | bytes 147464 | tf_op jit(solution)/shard_map/ppermute | solution.py:22
  199.1 19.2 %copy-start.94 = (f32[4,1,4,1,4,128]{5,4,2,0,1,3:T(4,128)S(1)}, f32[4,1,4,1,4,128]{5,4,2,0,1,3:T(4,128)}, u32[]{:S(2)}) copy-start(f32[4,1,4,1,4,128]{5,4,2,0,1,3:T(4,128)} %copy-done.93) | copy-start | bytes 98308
  204.5 13.8 %collective-permute-start.20 = (f32[4,9,4,1,4,128]{5,4,0,2,3,1:T(4,128)S(1)}, f32[4,9,4,1,4,128]{5,4,0,2,3,1:T(4,128)S(1)}, u32[]{:S(2)}, u32[]{:S(2)}) collective-permute-start(f32[4,9,4,1,4,128]{5,4,0,2,3,1:T(4,128)S(1)} %constant_dynamic-update-slice_fusion.9), channel_id=1, source_target_pairs={{0,16},{8,24},{16,0},{24,8},{1,17},{9,25},{17,1},{25,9},{2,18},{10... | collective-permute-start | bytes 884744 | tf_op jit(solution)/shard_map/ppermute | solution.py:28
  (70 other events, 434.7 us)
where the time goes:
time: 236 us; the launch traced here: 231 us
  other arithmetic  82.8 us (35%)
  local copies, waits for them, and re-layouts  66.3 us (28%)
  starting transfers between devices  44.6 us (19%)
  waiting for transfers between devices  31.3 us (13%)
  between operations  6.13 us (3%)
    ppermute x14, starting transfers between devices, shifted_2(): lax.ppermute(value, axis, [(i, (i + by) % devices) for i in range(devices)])  35 us
    gather x2, local copies, waits for them, and re-layouts, per_device(): noise_field = jnp.take(noise_table, noise_index, axis=3)  34.2 us
    ppermute x7, waiting for transfers between devices, partner_2(): return lax.ppermute(value, axis, pairs)  25.4 us
    unnamed x213, local copies, waits for them, and re-layouts  15.7 us
    reduce_sum x50, other arithmetic, mat_mat(): jnp.sum(left_real * right_real - left_imag * right_imag, axis=1)  10.7 us
    another operation x48, other arithmetic, spin_apply(): return jnp.stack([jnp.stack(rows_real), jnp.stack(rows_imag)])  10.2 us
    ppermute x7, starting transfers between devices, partner_2(): return lax.ppermute(value, axis, pairs)  9.65 us
    reduce_sum x13, other arithmetic, mat_vec(): out_real = jnp.sum(mat_real * vec_real - mat_imag * vec_imag, axis=2)  9.03 us
  transfers between devices with their start and end apart: 21, of which 6 were waited for; matrix products, arithmetic and copies ran while one was open for 19% of the time, Pallas kernels for 0%

commit v1 on v0

v1 whole, which is shorter than its diff:
```python
import functools

import jax
import jax.numpy as jnp
from jax import lax
from jax.experimental import pallas as pl
from jax.experimental.pallas import tpu as pltpu
from jax.sharding import PartitionSpec as P

MESH = pl.DeviceIdType.MESH
F32 = jnp.float32

MD_STEPS = 2

hopping = 0.13
step_size = 0.25
gamma_table = (
    ((3, 2, 1, 0), (0, 0, 0, 0), (1, 1, -1, -1)),
    ((2, 3, 0, 1), (1, 1, 1, 1), (0, 0, 0, 0)),
    ((3, 2, 1, 0), (-1, 1, 1, -1), (0, 0, 0, 0)),
    ((2, 3, 0, 1), (0, 0, 0, 0), (1, -1, -1, 1)),
)


def noise_kernel(table, index, out):
    rows, lanes = index.shape
    entries = table.shape[-1]
    lane = jnp.bitwise_and(index[...], lanes - 1)
    chunk = lax.div(index[...], lanes)

    def one(k, carry):
        for colour in range(3):
            total = jnp.zeros((rows, lanes), F32)
            for c in range(entries // lanes):
                row = table[k, colour : colour + 1, c * lanes : (c + 1) * lanes]
                value = jnp.take_along_axis(
                    jnp.broadcast_to(row, (rows, lanes)), lane, axis=1, mode="promise_in_bounds"
                )
                total = jnp.where(chunk == c, value, total)
            out[k, colour] = total
        return carry

    lax.fori_loop(0, 8, one, 0)


def times_i(re, im, g_re, g_im):
    if g_re == 1:
        return re, im
    if g_re == -1:
        return -re, -im
    if g_im == 1:
        return -im, re
    return im, -re


def project(spinor, mu, sign):
    order, g_re, g_im = gamma_table[mu]
    out_re, out_im = [], []
    for s in range(2):
        add_re, add_im = times_i(
            spinor[0, order[s]], spinor[1, order[s]], sign * g_re[s], sign * g_im[s]
        )
        out_re.append(spinor[0, s] + add_re)
        out_im.append(spinor[1, s] + add_im)
    return jnp.stack(out_re), jnp.stack(out_im)


def mat_vec(links, mu, half):
    re, im = half
    out_re = out_im = None
    for b in range(3):
        m_re, m_im = links[mu, 0, :, b][None], links[mu, 1, :, b][None]
        v_re, v_im = re[:, b : b + 1], im[:, b : b + 1]
        t_re = m_re * v_re - m_im * v_im
        t_im = m_re * v_im + m_im * v_re
        out_re = t_re if b == 0 else out_re + t_re
        out_im = t_im if b == 0 else out_im + t_im
    return out_re, out_im


def dag_vec(links, mu, half):
    re, im = half
    out_re = out_im = None
    for b in range(3):
        m_re, m_im = links[mu, 0, b][None], links[mu, 1, b][None]
        v_re, v_im = re[:, b : b + 1], im[:, b : b + 1]
        t_re = m_re * v_re + m_im * v_im
        t_im = m_re * v_im - m_im * v_re
        out_re = t_re if b == 0 else out_re + t_re
        out_im = t_im if b == 0 else out_im + t_im
    return out_re, out_im


def outer(first, second):
    out_re = out_im = None
    for s in range(2):
        f_re, f_im = first[0][s][:, None], first[1][s][:, None]
        g_re, g_im = second[0][s][None], second[1][s][None]
        t_re = f_re * g_re + f_im * g_im
        t_im = f_im * g_re - f_re * g_im
        out_re = t_re if s == 0 else out_re + t_re
        out_im = t_im if s == 0 else out_im + t_im
    return out_re, out_im


def complex_times(a, b):
    return a[0] * b[0] - a[1] * b[1], a[0] * b[1] + a[1] * b[0]


def complex_by_conj(a, b):
    return a[0] * b[0] + a[1] * b[1], a[1] * b[0] - a[0] * b[1]


def square(c):
    return c[0] * c[0] + c[1] * c[1]


def link_exponential(p):
    b = [step_size * part for part in p]
    d0, d1 = b[0], b[1]
    d2 = -(d0 + d1)
    o01, o02, o12 = (b[2], b[3]), (b[4], b[5]), (b[6], b[7])
    n01, n02, n12 = square(o01), square(o02), square(o12)
    s0 = d0 * d0 + n01 + n02
    s1 = d1 * d1 + n01 + n12
    s2 = d2 * d2 + n02 + n12
    r01 = complex_by_conj(o02, o12)
    r02 = complex_times(o01, o12)
    r12 = complex_times((o01[0], -o01[1]), o02)
    s01 = (r01[0] - d2 * o01[0], r01[1] - d2 * o01[1])
    s02 = (r02[0] - d1 * o02[0], r02[1] - d1 * o02[1])
    s12 = (r12[0] - d0 * o12[0], r12[1] - d0 * o12[1])
    c1 = 0.5 * (s0 + s1 + s2)
    c0 = (
        d0 * (d1 * d2 - n12) - d1 * n02 - d2 * n01
        + 2.0 * (r02[0] * o02[0] + r02[1] * o02[1])
    )
    q0 = (1.0 - c0 * c0 * (1.0 / 720.0), c0 * (c1 * (1.0 / 120.0) - 1.0 / 6.0))
    q1 = (c0 * (1.0 / 24.0 - c1 * (1.0 / 360.0)), 1.0 + c1 * (c1 * (1.0 / 120.0) - 1.0 / 6.0))
    q2 = (c1 * (1.0 / 24.0 - c1 * (1.0 / 720.0)) - 0.5, c0 * (1.0 / 120.0))
    e = [[None] * 3 for _ in range(3)]
    for k, (d, s) in enumerate(((d0, s0), (d1, s1), (d2, s2))):
        e[k][k] = (q0[0] + q1[0] * d + q2[0] * s, q0[1] + q1[1] * d + q2[1] * s)
    for i, j, o, s in ((0, 1, o01, s01), (0, 2, o02, s02), (1, 2, o12, s12)):
        a_re = q1[0] * o[0] + q2[0] * s[0]
        a_im = q1[0] * o[1] + q2[0] * s[1]
        b_re = q1[1] * o[0] + q2[1] * s[0]
        b_im = q1[1] * o[1] + q2[1] * s[1]
        e[i][j] = (a_re - b_im, a_im + b_re)
        e[j][i] = (a_re + b_im, b_re - a_im)
    return e


def kernel(
    n_xd, n_ta, u_in, m_in, noise, partner, u_out, m_out,
    h0, q0, h2, q2, phi, resp, acc, ahead, moved, f_perm, mom,
    face_out, face_in, time_out, time_in, force_out, force_in,
    face_s, face_r, time_s, time_r, force_s, force_r,
):
    n2 = face_in.shape[-2]
    rows, lanes = phi.shape[-2:]
    x1 = rows // n2
    xd, ta = lax.axis_index("xd"), lax.axis_index("ta")
    up = {"xd": lax.rem(xd + 1, n_xd)}
    down = {"xd": lax.rem(xd + n_xd - 1, n_xd)}
    mirror = {"xd": lax.rem(xd + n_xd // 2, n_xd)}
    later = {"ta": lax.rem(ta + 1, n_ta)}
    earlier = {"ta": lax.rem(ta + n_ta - 1, n_ta)}
    sign_ahead = jnp.where(ta == n_ta - 1, -1.0, 1.0).astype(F32)
    sign_behind = jnp.where(ta == 0, -1.0, 1.0).astype(F32)

    barrier = pltpu.get_barrier_semaphore()
    for other in (up, down, mirror, later, earlier):
        pl.semaphore_signal(barrier, inc=1, device_id=other, device_id_type=MESH)
    pl.semaphore_wait(barrier, 5)

    row = lax.broadcasted_iota(jnp.int32, (rows, lanes), 0)
    x_row = lax.div(row, n2)
    at_first = lax.rem(row, n2) == 0
    at_last = lax.rem(row, n2) == n2 - 1
    source_row = jnp.zeros((rows, lanes), jnp.int32)
    for x in range(x1):
        source_row = jnp.where(x_row == x, lax.rem(partner[x], x1), source_row)
    from_row = [source_row == x for x in range(x1)]
    turn = [source_row == lax.rem(x_row + d, x1) for d in range(x1)]

    def from_mirror(into, k, c):
        shape = into.shape[2:4] + (rows, lanes)
        taken = jnp.broadcast_to(into[k, c, :, :, 0:1], shape)
        for x in range(1, x1):
            other = jnp.broadcast_to(into[k, c, :, :, x : x + 1], shape)
            taken = jnp.where(from_row[x], other, taken)
        return taken

    sent = []
    count = {"face": 0, "time": 0}

    def send(kind, out, into, s_sem, r_sem, k, where):
        copy = pltpu.make_async_remote_copy(
            src_ref=out.at[k], dst_ref=into.at[k], send_sem=s_sem.at[k], recv_sem=r_sem.at[k],
            device_id=where, device_id_type=MESH,
        )
        copy.start()
        sent.append(copy)
        return copy, into, k

    def send_face(where):
        k = count["face"]
        count["face"] += 1
        return send("face", face_out, face_in, face_s, face_r, k, where)

    def send_time(where):
        k = count["time"]
        count["time"] += 1
        return send("time", time_out, time_in, time_s, time_r, k, where)

    def start_ahead(mu, half):
        for c in range(2):
            if mu == 0:
                h0[c, :, :, 0:rows] = half[c]
                face_out[count["face"], c] = half[c][:, :, 0:n2]
            elif mu == 1:
                time_out[count["time"], c] = half[c]
            elif mu == 2:
                h2[c, :, :, 0:rows] = half[c]
                for x in range(x1):
                    face_out[count["face"], c, :, :, x : x + 1] = half[c][:, :, x * n2 : x * n2 + 1]
        if mu == 0:
            return send_face(down)
        if mu == 1:
            return send_time(earlier)
        return send_face(mirror)

    def start_behind(mu, half):
        for c in range(2):
            if mu == 0:
                q0[c, :, :, 8 : 8 + rows] = half[c]
                face_out[count["face"], c] = half[c][:, :, rows - n2 : rows]
            elif mu == 1:
                time_out[count["time"], c] = half[c]
            elif mu == 2:
                q2[c, :, :, 8 : 8 + rows] = half[c]
                for x in range(x1):
                    last = x * n2 + n2 - 1
                    face_out[count["face"], c, :, :, x : x + 1] = half[c][:, :, last : last + 1]
        if mu == 0:
            return send_face(up)
        if mu == 1:
            return send_time(later)
        return send_face(mirror)

    def lane_roll(half, shift):
        return tuple(
            pltpu.roll(part.reshape(-1, lanes), shift, 1).reshape(part.shape) for part in half
        )

    def finish_ahead(mu, started, half=None):
        if mu == 3:
            return lane_roll(half, lanes - 1)
        copy, into, k = started
        copy.wait_recv()
        if mu == 0:
            h0[:, :, :, rows : rows + n2] = into[k]
            return tuple(h0[c, :, :, n2 : n2 + rows] for c in range(2))
        if mu == 1:
            return tuple(into[k, c] * sign_ahead for c in range(2))
        return tuple(
            jnp.where(at_last, from_mirror(into, k, c), h2[c, :, :, 1 : 1 + rows])
            for c in range(2)
        )

    def finish_behind(mu, started, half=None):
        if mu == 3:
            return lane_roll(half, 1)
        copy, into, k = started
        copy.wait_recv()
        if mu == 0:
            q0[:, :, :, 8 - n2 : 8] = into[k]
            return tuple(q0[c, :, :, 8 - n2 : 8 - n2 + rows] for c in range(2))
        if mu == 1:
            return tuple(into[k, c] * sign_behind for c in range(2))
        return tuple(
            jnp.where(at_first, from_mirror(into, k, c), q2[c, :, :, 7 : 7 + rows])
            for c in range(2)
        )

    def add_hop(mu, uh, qh, first):
        order, g_re, g_im = gamma_table[mu]
        total = [uh[c] + qh[c] for c in range(2)]
        diff = [uh[c] - qh[c] for c in range(2)]
        for c in range(2):
            upper = total[c]
            acc[c, 0:2] = upper if first else acc[c, 0:2] + upper
        for s in range(2, 4):
            low = times_i(diff[0][order[s]], diff[1][order[s]], g_re[s], g_im[s])
            for c in range(2):
                acc[c, s] = low[c] if first else acc[c, s] + low[c]

    def finish_spinor(source, out):
        out[...] = source[...] - hopping * acc[...]

    h2[:, :, :, rows : rows + 8] = jnp.zeros_like(h2[:, :, :, rows : rows + 8])
    q2[:, :, :, 0:8] = jnp.zeros_like(q2[:, :, :, 0:8])

    def dirac(source, out, links, keep, have_ahead, behind_ready=None):
        started_h, started_q = {}, {}
        for mu in (1, 2, 0):
            if not have_ahead:
                started_h[mu] = start_ahead(mu, project(source, mu, 1))
            if behind_ready is None:
                started_q[mu] = start_behind(mu, dag_vec(links, mu, project(source, mu, -1)))
            else:
                started_q[mu] = behind_ready[mu]
        first = True
        for mu in (3, 0, 2, 1):
            if have_ahead:
                half = tuple(ahead[mu, c] for c in range(2))
            else:
                half = finish_ahead(
                    mu, started_h.get(mu), project(source, mu, 1) if mu == 3 else None
                )
                if keep:
                    for c in range(2):
                        ahead[mu, c] = half[c]
            uh = mat_vec(links, mu, half)
            if keep:
                for c in range(2):
                    moved[mu, c] = uh[c]
            qh = finish_behind(
                mu, started_q.get(mu),
                dag_vec(links, mu, project(source, mu, -1)) if mu == 3 else None,
            )
            add_hop(mu, uh, qh, first)
            first = False
        finish_spinor(source, out)

    def force(mu, k, links, x_half):
        ux = mat_vec(links, mu, x_half)
        one = outer(ux, project(phi, mu, -1))
        two = outer(tuple(moved[mu, c] for c in range(2)), project(resp, mu, 1))
        g_re, g_im = one[0] + two[0], one[1] + two[1]
        scale = -2.0 * hopping
        third = (g_im[0, 0] + g_im[1, 1] + g_im[2, 2]) * (1.0 / 3.0)
        force_out[k, 0] = scale * (g_im[0, 0] - third)
        force_out[k, 1] = scale * (g_im[1, 1] - third)
        for n, (i, j) in enumerate(((0, 1), (0, 2), (1, 2))):
            force_out[k, 2 + 2 * n] = (0.5 * scale) * (g_im[i, j] + g_im[j, i])
            force_out[k, 3 + 2 * n] = (0.5 * scale) * (g_re[j, i] - g_re[i, j])
        return send("force", force_out, force_in, force_s, force_r, k, mirror)

    def update(mu, k, started, links, last):
        started[0].wait_recv()
        f_perm[:, 0:rows] = force_in[k]
        f_perm[:, rows : 2 * rows] = force_in[k]
        mirrored = f_perm[:, 0:rows]
        for d in range(1, x1):
            mirrored = jnp.where(turn[d], f_perm[:, d * n2 : d * n2 + rows], mirrored)
        p = []
        for n in range(8):
            real = n < 2 or n % 2 == 0
            here, there = force_out[k, n], mirrored[n]
            p.append(mom[mu, n] + step_size * (here - there if real else here + there))
        if last:
            zero = jnp.zeros((rows, lanes), F32)
            for n in range(3):
                m_out[mu, 0, n, n] = p[n] if n < 2 else -(p[0] + p[1])
                m_out[mu, 1, n, n] = zero
            for n, (i, j) in enumerate(((0, 1), (0, 2), (1, 2))):
                m_out[mu, 0, i, j] = p[2 + 2 * n]
                m_out[mu, 0, j, i] = p[2 + 2 * n]
                m_out[mu, 1, i, j] = p[3 + 2 * n]
                m_out[mu, 1, j, i] = -p[3 + 2 * n]
        else:
            for n in range(8):
                mom[mu, n] = p[n]
        e = link_exponential(p)
        u = [[(links[mu, 0, i, j], links[mu, 1, i, j]) for j in range(3)] for i in range(3)]
        for i in range(3):
            for j in range(3):
                parts = [complex_times(e[i][k2], u[k2][j]) for k2 in range(3)]
                for c in range(2):
                    u_out[mu, c, i, j] = parts[0][c] + parts[1][c] + parts[2][c]

    for mu in range(4):
        mom[mu, 0] = m_in[mu, 0, 0, 0]
        mom[mu, 1] = m_in[mu, 0, 1, 1]
        for n, (i, j) in enumerate(((0, 1), (0, 2), (1, 2))):
            mom[mu, 2 + 2 * n] = m_in[mu, 0, i, j]
            mom[mu, 3 + 2 * n] = m_in[mu, 1, i, j]

    dirac(noise, phi, u_in, False, False)
    behind_ready = None
    for step in range(MD_STEPS):
        links = u_in if step == 0 else u_out
        last = step == MD_STEPS - 1
        dirac(phi, resp, links, True, step > 0, behind_ready)
        started = {mu: start_ahead(mu, project(resp, mu, -1)) for mu in (1, 2, 0)}
        forces = {}
        for mu in (3, 0, 2, 1):
            x_half = finish_ahead(
                mu, started.get(mu), project(resp, mu, -1) if mu == 3 else None
            )
            forces[mu] = force(mu, 4 * step + mu, links, x_half)
        behind_ready = {}
        for mu in (3, 0, 2, 1):
            update(mu, 4 * step + mu, forces[mu], links, last)
            if not last and mu != 3:
                behind_ready[mu] = start_behind(mu, dag_vec(u_out, mu, project(phi, mu, -1)))
    for copy in sent:
        copy.wait_send()


def per_device(gauge_links, momenta, noise_table, noise_index, partner):
    lead = gauge_links.shape[:4]
    x1, n2, n3 = gauge_links.shape[4], gauge_links.shape[6], gauge_links.shape[7]
    rows = x1 * n2
    n_xd, n_ta = lax.axis_size("xd"), lax.axis_size("ta")
    noise = pl.pallas_call(
        noise_kernel,
        out_shape=jax.ShapeDtypeStruct((8, 3, rows, n3), F32),
    )(noise_table.reshape((8,) + noise_table.shape[2:]), noise_index.reshape(rows, n3))
    noise = noise.reshape(2, 4, 3, rows, n3)
    vmem = pl.BlockSpec(memory_space=pltpu.VMEM)
    half = (2, 2, 3)
    faces = 8 + 2 * MD_STEPS + 2 * (MD_STEPS - 1)
    times = 4 + MD_STEPS + (MD_STEPS - 1)
    field = (2, 4, 3, rows, n3)
    full = jax.ShapeDtypeStruct(lead + (rows, n3), F32)
    dma = pltpu.SemaphoreType.DMA
    new_links, new_momenta = pl.pallas_call(
        functools.partial(kernel, n_xd, n_ta),
        out_shape=(full, full),
        in_specs=[vmem, vmem, vmem, pl.BlockSpec(memory_space=pltpu.SMEM)],
        out_specs=(vmem, vmem),
        scratch_shapes=[
            pltpu.VMEM(half + (rows + 8, n3), F32),
            pltpu.VMEM(half + (rows + 8, n3), F32),
            pltpu.VMEM(half + (rows + 8, n3), F32),
            pltpu.VMEM(half + (rows + 8, n3), F32),
            pltpu.VMEM(field, F32),
            pltpu.VMEM(field, F32),
            pltpu.VMEM(field, F32),
            pltpu.VMEM((4,) + half + (rows, n3), F32),
            pltpu.VMEM((4,) + half + (rows, n3), F32),
            pltpu.VMEM((8, 2 * rows, n3), F32),
            pltpu.VMEM((4, 8, rows, n3), F32),
            pltpu.VMEM((faces,) + half + (n2, n3), F32),
            pltpu.VMEM((faces,) + half + (n2, n3), F32),
            pltpu.VMEM((times,) + half + (rows, n3), F32),
            pltpu.VMEM((times,) + half + (rows, n3), F32),
            pltpu.VMEM((4 * MD_STEPS, 8, rows, n3), F32),
            pltpu.VMEM((4 * MD_STEPS, 8, rows, n3), F32),
            dma((faces,)), dma((faces,)), dma((times,)), dma((times,)),
            dma((4 * MD_STEPS,)), dma((4 * MD_STEPS,)),
        ],
        compiler_params=pltpu.CompilerParams(
            collective_id=0, has_side_effects=True, vmem_limit_bytes=40 * 1024 * 1024
        ),
    )(
        gauge_links.reshape(lead + (rows, n3)), momenta.reshape(lead + (rows, n3)), noise, partner
    )
    return new_links.reshape(gauge_links.shape), new_momenta.reshape(momenta.shape)


def solution(mesh):
    placed = (
        P(None, None, None, None, "xd", "ta", None, None),
        P(None, None, None, None, "xd", "ta", None, None),
        P(),
        P("xd", "ta", None, None),
        P("xd"),
    )
    return jax.shard_map(
        per_device,
        mesh=mesh,
        in_specs=placed,
        out_specs=(
            P(None, None, None, None, "xd", "ta", None, None),
            P(None, None, None, None, "xd", "ta", None, None),
        ),
        check_vma=False,
    )
```

time: 236 us -> 57.5 us (0.24); the launches traced: 231 us -> 57.3 us
  other arithmetic: 82.8 us -> 0 us
  local copies, waits for them, and re-layouts: 66.3 us -> 5.34 us
  Pallas kernels: 0 us -> 51.3 us
  starting transfers between devices: 44.6 us -> 0 us
  waiting for transfers between devices: 31.3 us -> 0 us
  between operations: 6.13 us -> 0.65 us
    pallas_call x0 -> x2, Pallas kernels: none -> 51.3 us  [the longest x1 47.3 us: per_device(): pl.pallas_call(functools.partial(kernel, n_xd, n_ta), out_shape=(full, fu...]
    ppermute x21 -> x0, starting transfers between devices: 44.6 us -> none  [the longest x14 35 us: shifted_2(): lax.ppermute(value, axis, [(i, (i + by) % devices) for i in range(devices)])]
    gather x9 -> x0, local copies, waits for them, and re-layouts: 41.9 us -> none  [the longest x2 34.2 us: per_device(): noise_field = jnp.take(noise_table, noise_index, axis=3)]
    ppermute x21 -> x0, waiting for transfers between devices: 31.3 us -> none  [the longest x7 25.4 us: partner_2(): return lax.ppermute(value, axis, pairs)]
    reduce_sum x81 -> x0, other arithmetic: 30 us -> none  [the longest x50 10.7 us: mat_mat(): jnp.sum(left_real * right_real - left_imag * right_imag, axis=1)]
    another operation x83 -> x0, other arithmetic: 13.9 us -> none  [the longest x48 10.2 us: spin_apply(): return jnp.stack([jnp.stack(rows_real), jnp.stack(rows_imag)])]
    add x125 -> x0, other arithmetic: 13.4 us -> none  [the longest x8 4.21 us: force_term(): outer_sum(ahead_field, phi) + outer_sum(phi_ahead[direction], local_field)]
    unnamed x213 -> x11, local copies, waits for them, and re-layouts: 15.7 us -> 5.34 us
  transfers between devices with their start and end apart: 21 -> 0, of which waited for: 6 -> 0; matrix products, arithmetic and copies ran while one was open for 19% -> 0% of each run, Pallas kernels for 0% -> 0%
where the time goes in v1:
time: 57.5 us; the launch traced here: 57.3 us
  Pallas kernels  51.3 us (89%)
  local copies, waits for them, and re-layouts  5.34 us (9%)
  between operations  0.65 us (1%)
    pallas_call x1, Pallas kernels, per_device(): pl.pallas_call(functools.partial(kernel, n_xd, n_ta), out_shape=(full, fu...  47.3 us
    unnamed x11, local copies, waits for them, and re-layouts  5.34 us
    pallas_call x1, Pallas kernels, per_device(): pl.pallas_call(noise_kernel, out_shape=jax.ShapeDtypeStruct((8, 3, rows,...  4 us

profile of v1, /device:TPU:0, one launch (start us, length us, event | category | flops | bytes accessed | tf_op | source)
XLA Modules:
  0.0 57.3 jit_solution(18267779499376925864)
XLA Ops:
  0.6 0.0 copy-start.2
  0.6 2.1 %copy.7 = f32[2,4,3,4096]{3,2,1,0:T(4,128)} copy(f32[2,4,3,4096]{3,1,2,0:T(4,128)} %param.7) | data formatting | bytes 786432 | tf_op args[2]
  2.8 0.0 copy-start.1
  2.8 4.0 %shard_map.68 = f32[8,3,16,128]{3,2,1,0:T(8,128)} custom-call(f32[8,3,4096]{2,1,0:T(4,128)} %bitcast.16, s32[16,128]{1,0:T(8,128)} %bitcast.17), custom_call_target="tpu_custom_call" | custom-call | tf_op jit(solution)/shard_map/pallas_call | solution.py:418
  6.8 0.0 copy-start.3
  6.8 0.0 copy-done.2
  6.8 0.0 copy-done.1
  6.8 0.6 %copy-done.3 = s32[4]{0:T(128)S(1)} copy-done((s32[4]{0:T(128)S(1)}, s32[4]{0:T(128)}, u32[]{:S(2)}) %copy-start.3) | copy-done | bytes 40
  7.4 0.0 copy-start
  7.4 0.9 %copy-done = f32[8,3,16,128]{3,2,1,0:T(8,128)S(1)} copy-done((f32[8,3,16,128]{3,2,1,0:T(8,128)S(1)}, f32[8,3,16,128]{3,2,1,0:T(8,128)}, u32[]{:S(2)}) %copy-start) | copy-done | bytes 196632
  8.3 47.3 %shard_map.69 = (f32[4,2,3,3,16,128]{5,4,3,2,1,0:T(8,128)S(1)}, f32[4,2,3,3,16,128]{5,4,3,2,1,0:T(8,128)S(1)}) custom-call(f32[4,2,3,3,16,128]{5,4,3,2,1,0:T(8,128)S(1)} %bitcast.12, f32[4,2,3,3,16,128]{5,4,3,2,1,0:T(8,128)S(1)} %bitcast.13, f32[2,4,3,16,128]{4,3,2,1,0:T(8,128)S(1)} %bitcast.11, s32[4]{0:T(128)S(1)} %copy-done.3), custom_call_target="tpu_custom_call" | custom-call | tf_op jit(solution)/shard_map/pallas_call | solution.py:430
  55.7 0.8 %copy.12 = f32[4,2,3,3,4,1,4,128]{7,6,5,4,3,2,1,0:T(4,128)} copy(f32[4,2,3,3,4,1,4,128]{7,6,5,4,3,2,1,0:T(4,128)S(1)} %bitcast.15) | data formatting | bytes 1179648
  56.5 0.8 %copy.13 = f32[4,2,3,3,4,1,4,128]{7,6,5,4,3,2,1,0:T(4,128)} copy(f32[4,2,3,3,4,1,4,128]{7,6,5,4,3,2,1,0:T(4,128)S(1)} %bitcast.14) | data formatting | bytes 1179648
Async XLA Ops:
  0.6 6.1 %copy-start.2 = (f32[4,2,3,3,4,1,4,128]{7,6,5,4,3,2,1,0:T(4,128)S(1)}, f32[4,2,3,3,4,1,4,128]{7,6,5,4,3,2,1,0:T(4,128)}, u32[]{:S(2)}) copy-start(f32[4,2,3,3,4,1,4,128]{7,6,5,4,3,2,1,0:T(4,128)} %param.6) | copy-start | bytes 1769476
  2.8 4.0 %copy-start.1 = (f32[4,2,3,3,4,1,4,128]{7,6,5,4,3,2,1,0:T(4,128)S(1)}, f32[4,2,3,3,4,1,4,128]{7,6,5,4,3,2,1,0:T(4,128)}, u32[]{:S(2)}) copy-start(f32[4,2,3,3,4,1,4,128]{7,6,5,4,3,2,1,0:T(4,128)} %param.5) | copy-start | bytes 1769476
  6.8 0.7 %copy-start.3 = (s32[4]{0:T(128)S(1)}, s32[4]{0:T(128)}, u32[]{:S(2)}) copy-start(s32[4]{0:T(128)} %partner.1) | copy-start | bytes 52
  7.4 0.9 %copy-start = (f32[8,3,16,128]{3,2,1,0:T(8,128)S(1)}, f32[8,3,16,128]{3,2,1,0:T(8,128)}, u32[]{:S(2)}) copy-start(f32[8,3,16,128]{3,2,1,0:T(8,128)} %shard_map.68) | copy-start | bytes 589828

commit v2 on v1

--- a/solution.py
+++ b/solution.py
@@ -22,25 +22,26 @@
 )
 
 
-def noise_kernel(table, index, out):
+def gather_noise(table, index, out):
     rows, lanes = index.shape
     entries = table.shape[-1]
     lane = jnp.bitwise_and(index[...], lanes - 1)
     chunk = lax.div(index[...], lanes)
 
     def one(k, carry):
-        for colour in range(3):
+        part, colour = lax.div(k, 3), lax.rem(k, 3)
+        for spin in range(4):
             total = jnp.zeros((rows, lanes), F32)
             for c in range(entries // lanes):
-                row = table[k, colour : colour + 1, c * lanes : (c + 1) * lanes]
+                row = table[part, colour, spin : spin + 1, c * lanes : (c + 1) * lanes]
                 value = jnp.take_along_axis(
                     jnp.broadcast_to(row, (rows, lanes)), lane, axis=1, mode="promise_in_bounds"
                 )
                 total = jnp.where(chunk == c, value, total)
-            out[k, colour] = total
+            out[part, spin, colour] = total
         return carry
 
-    lax.fori_loop(0, 8, one, 0)
+    lax.fori_loop(0, 6, one, 0)
 
 
 def times_i(re, im, g_re, g_im):
@@ -152,10 +153,11 @@
 
 
 def kernel(
-    n_xd, n_ta, u_in, m_in, noise, partner, u_out, m_out,
+    n_xd, n_ta, u_hbm, m_hbm, table, index, partner, u_out, m_out,
+    u_in, m_in, noise,
     h0, q0, h2, q2, phi, resp, acc, ahead, moved, f_perm, mom,
     face_out, face_in, time_out, time_in, force_out, force_in,
-    face_s, face_r, time_s, time_r, force_s, force_r,
+    face_s, face_r, time_s, time_r, force_s, force_r, load_s,
 ):
     n2 = face_in.shape[-2]
     rows, lanes = phi.shape[-2:]
@@ -172,7 +174,15 @@
     barrier = pltpu.get_barrier_semaphore()
     for other in (up, down, mirror, later, earlier):
         pl.semaphore_signal(barrier, inc=1, device_id=other, device_id_type=MESH)
+    loads = [
+        pltpu.make_async_copy(u_hbm, u_in, load_s.at[0]),
+        pltpu.make_async_copy(m_hbm, m_in, load_s.at[1]),
+    ]
+    for load in loads:
+        load.start()
+    gather_noise(table, index, noise)
     pl.semaphore_wait(barrier, 5)
+    loads[0].wait()
 
     row = lax.broadcasted_iota(jnp.int32, (rows, lanes), 0)
     x_row = lax.div(row, n2)
@@ -284,15 +294,12 @@
             for c in range(2)
         )
 
-    def add_hop(mu, uh, qh, first):
+    def add_hop(mu, half, sign, first=False):
         order, g_re, g_im = gamma_table[mu]
-        total = [uh[c] + qh[c] for c in range(2)]
-        diff = [uh[c] - qh[c] for c in range(2)]
         for c in range(2):
-            upper = total[c]
-            acc[c, 0:2] = upper if first else acc[c, 0:2] + upper
+            acc[c, 0:2] = half[c] if first else acc[c, 0:2] + half[c]
         for s in range(2, 4):
-            low = times_i(diff[0][order[s]], diff[1][order[s]], g_re[s], g_im[s])
+            low = times_i(half[0][order[s]], half[1][order[s]], sign * g_re[s], sign * g_im[s])
             for c in range(2):
                 acc[c, s] = low[c] if first else acc[c, s] + low[c]
 
@@ -302,37 +309,29 @@
     h2[:, :, :, rows : rows + 8] = jnp.zeros_like(h2[:, :, :, rows : rows + 8])
     q2[:, :, :, 0:8] = jnp.zeros_like(q2[:, :, :, 0:8])
 
-    def dirac(source, out, links, keep, have_ahead, behind_ready=None):
+    def local_hop(links, source, mu, half, keep, first):
+        uh = mat_vec(links, mu, half)
+        if keep:
+            for c in range(2):
+                moved[mu, c] = uh[c]
+        add_hop(mu, uh, 1, first)
+
+    def dirac(source, out, links, keep):
         started_h, started_q = {}, {}
-        for mu in (1, 2, 0):
-            if not have_ahead:
-                started_h[mu] = start_ahead(mu, project(source, mu, 1))
-            if behind_ready is None:
-                started_q[mu] = start_behind(mu, dag_vec(links, mu, project(source, mu, -1)))
-            else:
-                started_q[mu] = behind_ready[mu]
-        first = True
-        for mu in (3, 0, 2, 1):
-            if have_ahead:
-                half = tuple(ahead[mu, c] for c in range(2))
-            else:
-                half = finish_ahead(
-                    mu, started_h.get(mu), project(source, mu, 1) if mu == 3 else None
-                )
-                if keep:
-                    for c in range(2):
-                        ahead[mu, c] = half[c]
-            uh = mat_vec(links, mu, half)
+        for mu in (2, 1, 0):
+            started_h[mu] = start_ahead(mu, project(source, mu, 1))
+            started_q[mu] = start_behind(mu, dag_vec(links, mu, project(source, mu, -1)))
+        for mu in (3, 0, 1, 2):
+            half = finish_ahead(mu, started_h.get(mu), project(source, mu, 1) if mu == 3 else None)
             if keep:
                 for c in range(2):
-                    moved[mu, c] = uh[c]
-            qh = finish_behind(
-                mu, started_q.get(mu),
-                dag_vec(links, mu, project(source, mu, -1)) if mu == 3 else None,
-            )
-            add_hop(mu, uh, qh, first)
-            first = False
+                    ahead[mu, c] = half[c]
+            local_hop(links, source, mu, half, keep, mu == 3)
+            qh = dag_vec(links, mu, project(source, mu, -1)) if mu == 3 else None
+            add_hop(mu, finish_behind(mu, started_q.get(mu), qh), -1)
         finish_spinor(source, out)
+
+    early = 6
 
     def force(mu, k, links, x_half):
         ux = mat_vec(links, mu, x_half)
@@ -346,10 +345,21 @@
         for n, (i, j) in enumerate(((0, 1), (0, 2), (1, 2))):
             force_out[k, 2 + 2 * n] = (0.5 * scale) * (g_im[i, j] + g_im[j, i])
             force_out[k, 3 + 2 * n] = (0.5 * scale) * (g_re[j, i] - g_re[i, j])
-        return send("force", force_out, force_in, force_s, force_r, k, mirror)
+
+    def send_force(k, piece):
+        rows_of = (pl.ds(0, early), pl.ds(early, 8 - early), pl.ds(0, 8))[piece]
+        copy = pltpu.make_async_remote_copy(
+            src_ref=force_out.at[k, rows_of], dst_ref=force_in.at[k, rows_of],
+            send_sem=force_s.at[k, piece], recv_sem=force_r.at[k, piece],
+            device_id=mirror, device_id_type=MESH,
+        )
+        copy.start()
+        sent.append(copy)
+        return copy
 
     def update(mu, k, started, links, last):
-        started[0].wait_recv()
+        for copy in started:
+            copy.wait_recv()
         f_perm[:, 0:rows] = force_in[k]
         f_perm[:, rows : 2 * rows] = force_in[k]
         mirrored = f_perm[:, 0:rows]
@@ -381,31 +391,43 @@
                 for c in range(2):
                     u_out[mu, c, i, j] = parts[0][c] + parts[1][c] + parts[2][c]
 
+    dirac(noise, phi, u_in, False)
+    dirac(phi, resp, u_in, True)
+    loads[1].wait()
     for mu in range(4):
         mom[mu, 0] = m_in[mu, 0, 0, 0]
         mom[mu, 1] = m_in[mu, 0, 1, 1]
         for n, (i, j) in enumerate(((0, 1), (0, 2), (1, 2))):
             mom[mu, 2 + 2 * n] = m_in[mu, 0, i, j]
             mom[mu, 3 + 2 * n] = m_in[mu, 1, i, j]
-
-    dirac(noise, phi, u_in, False, False)
-    behind_ready = None
     for step in range(MD_STEPS):
         links = u_in if step == 0 else u_out
         last = step == MD_STEPS - 1
-        dirac(phi, resp, links, True, step > 0, behind_ready)
-        started = {mu: start_ahead(mu, project(resp, mu, -1)) for mu in (1, 2, 0)}
+        started = {mu: start_ahead(mu, project(resp, mu, -1)) for mu in (2, 1, 0)}
         forces = {}
-        for mu in (3, 0, 2, 1):
+        for mu in (3, 0, 1, 2):
             x_half = finish_ahead(
                 mu, started.get(mu), project(resp, mu, -1) if mu == 3 else None
             )
-            forces[mu] = force(mu, 4 * step + mu, links, x_half)
-        behind_ready = {}
-        for mu in (3, 0, 2, 1):
+            force(mu, 4 * step + mu, links, x_half)
+            forces[mu] = [send_force(4 * step + mu, 0 if mu == 3 else 2)]
+        forces[3].append(send_force(4 * step + 3, 1))
+        behind = {}
+        for mu in (0, 1, 2, 3):
             update(mu, 4 * step + mu, forces[mu], links, last)
-            if not last and mu != 3:
-                behind_ready[mu] = start_behind(mu, dag_vec(u_out, mu, project(phi, mu, -1)))
+            if last:
+                continue
+            qh = dag_vec(u_out, mu, project(phi, mu, -1))
+            if mu != 3:
+                behind[mu] = start_behind(mu, qh)
+            else:
+                add_hop(mu, finish_behind(mu, None, qh), -1)
+            half = tuple(ahead[mu, c] for c in range(2))
+            local_hop(u_out, phi, mu, half, True, mu == 0)
+        if not last:
+            for mu in (0, 1, 2):
+                add_hop(mu, finish_behind(mu, behind[mu]), -1)
+            finish_spinor(phi, resp)
     for copy in sent:
         copy.wait_send()
 
@@ -415,12 +437,8 @@
     x1, n2, n3 = gauge_links.shape[4], gauge_links.shape[6], gauge_links.shape[7]
     rows = x1 * n2
     n_xd, n_ta = lax.axis_size("xd"), lax.axis_size("ta")
-    noise = pl.pallas_call(
-        noise_kernel,
-        out_shape=jax.ShapeDtypeStruct((8, 3, rows, n3), F32),
-    )(noise_table.reshape((8,) + noise_table.shape[2:]), noise_index.reshape(rows, n3))
-    noise = noise.reshape(2, 4, 3, rows, n3)
     vmem = pl.BlockSpec(memory_space=pltpu.VMEM)
+    hbm = pl.BlockSpec(memory_space=pltpu.HBM)
     half = (2, 2, 3)
     faces = 8 + 2 * MD_STEPS + 2 * (MD_STEPS - 1)
     times = 4 + MD_STEPS + (MD_STEPS - 1)
@@ -430,9 +448,12 @@
     new_links, new_momenta = pl.pallas_call(
         functools.partial(kernel, n_xd, n_ta),
         out_shape=(full, full),
-        in_specs=[vmem, vmem, vmem, pl.BlockSpec(memory_space=pltpu.SMEM)],
+        in_specs=[hbm, hbm, vmem, vmem, pl.BlockSpec(memory_space=pltpu.SMEM)],
         out_specs=(vmem, vmem),
         scratch_shapes=[
+            pltpu.VMEM(lead + (rows, n3), F32),
+            pltpu.VMEM(lead + (rows, n3), F32),
+            pltpu.VMEM(field, F32),
             pltpu.VMEM(half + (rows + 8, n3), F32),
             pltpu.VMEM(half + (rows + 8, n3), F32),
             pltpu.VMEM(half + (rows + 8, n3), F32),
@@ -451,13 +472,15 @@
             pltpu.VMEM((4 * MD_STEPS, 8, rows, n3), F32),
             pltpu.VMEM((4 * MD_STEPS, 8, rows, n3), F32),
             dma((faces,)), dma((faces,)), dma((times,)), dma((times,)),
-            dma((4 * MD_STEPS,)), dma((4 * MD_STEPS,)),
+            dma((4 * MD_STEPS, 3)), dma((4 * MD_STEPS, 3)),
+            dma((2,)),
         ],
         compiler_params=pltpu.CompilerParams(
             collective_id=0, has_side_effects=True, vmem_limit_bytes=40 * 1024 * 1024
         ),
     )(
-        gauge_links.reshape(lead + (rows, n3)), momenta.reshape(lead + (rows, n3)), noise, partner
+        gauge_links.reshape(lead + (rows, n3)), momenta.reshape(lead + (rows, n3)),
+        jnp.swapaxes(noise_table, 1, 2), noise_index.reshape(rows, n3), partner,
     )
     return new_links.reshape(gauge_links.shape), new_momenta.reshape(momenta.shape)
 

time: 57.5 us -> 54.8 us (0.953)
  Pallas kernels: 51.3 us -> 47.7 us
  local copies, waits for them, and re-layouts: 5.34 us -> 6.1 us
    pallas_call x1 -> x0, Pallas kernels: 4 us -> none  [per_device(): pl.pallas_call(noise_kernel, out_shape=jax.ShapeDtypeStruct((8, 3, rows,...]
    unnamed x11 -> x12, local copies, waits for them, and re-layouts: 5.34 us -> 6.1 us
where the time goes in v2:
time: 54.8 us; the launch traced here: 54.5 us
  Pallas kernels  47.7 us (87%)
  local copies, waits for them, and re-layouts  6.1 us (11%)
  between operations  0.65 us (1%)
    pallas_call x1, Pallas kernels, per_device(): pl.pallas_call(functools.partial(kernel, n_xd, n_ta), out_shape=(full, fu...  47.7 us
    unnamed x12, local copies, waits for them, and re-layouts  6.1 us

profile of v2, /device:TPU:0, one launch (start us, length us, event | category | flops | bytes accessed | tf_op | source)
XLA Modules:
  0.0 54.5 jit_solution(16635994989421279175)
XLA Ops:
  0.6 0.0 copy-start.4
  0.6 0.6 %copy-done.4 = s32[4]{0:T(128)S(1)} copy-done((s32[4]{0:T(128)S(1)}, s32[4]{0:T(128)}, u32[]{:S(2)}) %copy-start.4) | copy-done | bytes 40
  1.3 0.0 copy-start
  1.3 1.1 %copy-done = f32[4,2,3,3,4,1,4,128]{7,6,5,4,3,2,1,0:T(4,128)S(1)} copy-done((f32[4,2,3,3,4,1,4,128]{7,6,5,4,3,2,1,0:T(4,128)S(1)}, f32[4,2,3,3,4,1,4,128]{7,6,5,4,3,2,1,0:T(4,128)}, u32[]{:S(2)}) %copy-start) | copy-done | bytes 589848
  2.4 0.0 copy-start.1
  2.4 1.1 %copy-done.1 = f32[4,2,3,3,4,1,4,128]{7,6,5,4,3,2,1,0:T(4,128)S(1)} copy-done((f32[4,2,3,3,4,1,4,128]{7,6,5,4,3,2,1,0:T(4,128)S(1)}, f32[4,2,3,3,4,1,4,128]{7,6,5,4,3,2,1,0:T(4,128)}, u32[]{:S(2)}) %copy-start.1) | copy-done | bytes 589848
  3.4 0.0 copy-start.2
  3.4 1.0 %copy-done.2 = f32[2,4,3,4096]{3,1,2,0:T(4,128)S(1)} copy-done((f32[2,4,3,4096]{3,1,2,0:T(4,128)S(1)}, f32[2,4,3,4096]{3,1,2,0:T(4,128)}, u32[]{:S(2)}) %copy-start.2) | copy-done | bytes 393240
  4.4 0.0 copy-start.3
  4.4 0.7 %copy-done.3 = s32[4,1,4,128]{3,2,1,0:T(4,128)S(1)} copy-done((s32[4,1,4,128]{3,2,1,0:T(4,128)S(1)}, s32[4,1,4,128]{3,2,1,0:T(4,128)}, u32[]{:S(2)}) %copy-start.3) | copy-done | bytes 8216
  5.1 47.7 %shard_map.68 = (f32[4,2,3,3,16,128]{5,4,3,2,1,0:T(8,128)S(1)}, f32[4,2,3,3,16,128]{5,4,3,2,1,0:T(8,128)S(1)}) custom-call(f32[4,2,3,3,16,128]{5,4,3,2,1,0:T(8,128)S(1)} %bitcast.10, f32[4,2,3,3,16,128]{5,4,3,2,1,0:T(8,128)S(1)} %bitcast.11, f32[2,3,4,4096]{3,2,1,0:T(4,128)S(1)} %bitcast.14, s32[16,128]{1,0:T(8,128)S(1)} %bitcast.15, s32[4]{0:T(128)S(1)} %copy-done.4), custom_call_target="tpu_custom_call" | custom-call | tf_op jit(solution)/shard_map/pallas_call | solution.py:448
  52.8 0.8 %copy.11 = f32[4,2,3,3,4,1,4,128]{7,6,5,4,3,2,1,0:T(4,128)} copy(f32[4,2,3,3,4,1,4,128]{7,6,5,4,3,2,1,0:T(4,128)S(1)} %bitcast.13) | data formatting | bytes 1179648
  53.6 0.8 %copy.12 = f32[4,2,3,3,4,1,4,128]{7,6,5,4,3,2,1,0:T(4,128)} copy(f32[4,2,3,3,4,1,4,128]{7,6,5,4,3,2,1,0:T(4,128)S(1)} %bitcast.12) | data formatting | bytes 1179648
Async XLA Ops:
  0.6 0.7 %copy-start.4 = (s32[4]{0:T(128)S(1)}, s32[4]{0:T(128)}, u32[]{:S(2)}) copy-start(s32[4]{0:T(128)} %partner.1) | copy-start | bytes 52
  1.3 1.1 %copy-start = (f32[4,2,3,3,4,1,4,128]{7,6,5,4,3,2,1,0:T(4,128)S(1)}, f32[4,2,3,3,4,1,4,128]{7,6,5,4,3,2,1,0:T(4,128)}, u32[]{:S(2)}) copy-start(f32[4,2,3,3,4,1,4,128]{7,6,5,4,3,2,1,0:T(4,128)} %param.5) | copy-start | bytes 1769476
  2.4 1.1 %copy-start.1 = (f32[4,2,3,3,4,1,4,128]{7,6,5,4,3,2,1,0:T(4,128)S(1)}, f32[4,2,3,3,4,1,4,128]{7,6,5,4,3,2,1,0:T(4,128)}, u32[]{:S(2)}) copy-start(f32[4,2,3,3,4,1,4,128]{7,6,5,4,3,2,1,0:T(4,128)} %param.6) | copy-start | bytes 1769476
  3.4 1.0 %copy-start.2 = (f32[2,4,3,4096]{3,1,2,0:T(4,128)S(1)}, f32[2,4,3,4096]{3,1,2,0:T(4,128)}, u32[]{:S(2)}) copy-start(f32[2,4,3,4096]{3,1,2,0:T(4,128)} %param.7) | copy-start | bytes 1179652
  4.4 0.7 %copy-start.3 = (s32[4,1,4,128]{3,2,1,0:T(4,128)S(1)}, s32[4,1,4,128]{3,2,1,0:T(4,128)}, u32[]{:S(2)}) copy-start(s32[4,1,4,128]{3,2,1,0:T(4,128)} %param.8) | copy-start | bytes 24580

commit v3 on v2

--- a/solution.py
+++ b/solution.py
@@ -153,11 +153,11 @@
 
 
 def kernel(
-    n_xd, n_ta, u_hbm, m_hbm, table, index, partner, u_out, m_out,
-    u_in, m_in, noise,
+    n_xd, n_ta, u_hbm, m_hbm, table_hbm, index_hbm, partner, u_final, m_final,
+    u_in, m_in, table, index, u_out, m_out, noise,
     h0, q0, h2, q2, phi, resp, acc, ahead, moved, f_perm, mom,
     face_out, face_in, time_out, time_in, force_out, force_in,
-    face_s, face_r, time_s, time_r, force_s, force_r, load_s,
+    face_s, face_r, time_s, time_r, force_s, force_r, load_s, store_s,
 ):
     n2 = face_in.shape[-2]
     rows, lanes = phi.shape[-2:]
@@ -171,15 +171,19 @@
     sign_ahead = jnp.where(ta == n_ta - 1, -1.0, 1.0).astype(F32)
     sign_behind = jnp.where(ta == 0, -1.0, 1.0).astype(F32)
 
+    loads = [
+        pltpu.make_async_copy(u_hbm, u_in, load_s.at[0]),
+        pltpu.make_async_copy(m_hbm, m_in, load_s.at[1]),
+        pltpu.make_async_copy(table_hbm, table, load_s.at[2]),
+        pltpu.make_async_copy(index_hbm, index, load_s.at[3]),
+    ]
+    for n in (3, 2, 0, 1):
+        loads[n].start()
     barrier = pltpu.get_barrier_semaphore()
     for other in (up, down, mirror, later, earlier):
         pl.semaphore_signal(barrier, inc=1, device_id=other, device_id_type=MESH)
-    loads = [
-        pltpu.make_async_copy(u_hbm, u_in, load_s.at[0]),
-        pltpu.make_async_copy(m_hbm, m_in, load_s.at[1]),
-    ]
-    for load in loads:
-        load.start()
+    loads[3].wait()
+    loads[2].wait()
     gather_noise(table, index, noise)
     pl.semaphore_wait(barrier, 5)
     loads[0].wait()
@@ -202,7 +206,7 @@
             taken = jnp.where(from_row[x], other, taken)
         return taken
 
-    sent = []
+    sent, stores = [], []
     count = {"face": 0, "time": 0}
 
     def send(kind, out, into, s_sem, r_sem, k, where):
@@ -416,6 +420,10 @@
         for mu in (0, 1, 2, 3):
             update(mu, 4 * step + mu, forces[mu], links, last)
             if last:
+                for n, (value, final) in enumerate(((u_out, u_final), (m_out, m_final))):
+                    copy = pltpu.make_async_copy(value.at[mu], final.at[mu], store_s.at[mu, n])
+                    copy.start()
+                    stores.append(copy)
                 continue
             qh = dag_vec(u_out, mu, project(phi, mu, -1))
             if mu != 3:
@@ -430,6 +438,20 @@
             finish_spinor(phi, resp)
     for copy in sent:
         copy.wait_send()
+    for copy in stores:
+        copy.wait()
+
+
+def hand_over(links, momenta, links_out, momenta_out, sems):
+    copies = [
+        pltpu.make_async_copy(source.at[mu], out.at[mu], sems.at[n, mu])
+        for mu in range(4)
+        for n, (source, out) in enumerate(((links, links_out), (momenta, momenta_out)))
+    ]
+    for copy in copies:
+        copy.start()
+    for copy in copies:
+        copy.wait()
 
 
 def per_device(gauge_links, momenta, noise_table, noise_index, partner):
@@ -437,7 +459,6 @@
     x1, n2, n3 = gauge_links.shape[4], gauge_links.shape[6], gauge_links.shape[7]
     rows = x1 * n2
     n_xd, n_ta = lax.axis_size("xd"), lax.axis_size("ta")
-    vmem = pl.BlockSpec(memory_space=pltpu.VMEM)
     hbm = pl.BlockSpec(memory_space=pltpu.HBM)
     half = (2, 2, 3)
     faces = 8 + 2 * MD_STEPS + 2 * (MD_STEPS - 1)
@@ -448,9 +469,13 @@
     new_links, new_momenta = pl.pallas_call(
         functools.partial(kernel, n_xd, n_ta),
         out_shape=(full, full),
-        in_specs=[hbm, hbm, vmem, vmem, pl.BlockSpec(memory_space=pltpu.SMEM)],
-        out_specs=(vmem, vmem),
+        in_specs=[hbm, hbm, hbm, hbm, pl.BlockSpec(memory_space=pltpu.SMEM)],
+        out_specs=(hbm, hbm),
         scratch_shapes=[
+            pltpu.VMEM(lead + (rows, n3), F32),
+            pltpu.VMEM(lead + (rows, n3), F32),
+            pltpu.VMEM(noise_table.shape[:1] + (3, 4) + noise_table.shape[3:], F32),
+            pltpu.VMEM((rows, n3), jnp.int32),
             pltpu.VMEM(lead + (rows, n3), F32),
             pltpu.VMEM(lead + (rows, n3), F32),
             pltpu.VMEM(field, F32),
@@ -473,15 +498,22 @@
             pltpu.VMEM((4 * MD_STEPS, 8, rows, n3), F32),
             dma((faces,)), dma((faces,)), dma((times,)), dma((times,)),
             dma((4 * MD_STEPS, 3)), dma((4 * MD_STEPS, 3)),
-            dma((2,)),
+            dma((4,)), dma((4, 2)),
         ],
         compiler_params=pltpu.CompilerParams(
-            collective_id=0, has_side_effects=True, vmem_limit_bytes=40 * 1024 * 1024
+            collective_id=0, has_side_effects=True, vmem_limit_bytes=60 * 1024 * 1024
         ),
     )(
         gauge_links.reshape(lead + (rows, n3)), momenta.reshape(lead + (rows, n3)),
         jnp.swapaxes(noise_table, 1, 2), noise_index.reshape(rows, n3), partner,
     )
+    new_links, new_momenta = pl.pallas_call(
+        hand_over,
+        out_shape=(full, full),
+        in_specs=[hbm, hbm],
+        out_specs=(hbm, hbm),
+        scratch_shapes=[dma((2, 4))],
+    )(new_links, new_momenta)
     return new_links.reshape(gauge_links.shape), new_momenta.reshape(momenta.shape)
 
 

time: 54.8 us -> 87.2 us (1.59)
  Pallas kernels: 47.7 us -> 86.4 us
  local copies, waits for them, and re-layouts: 6.1 us -> 0 us
    pallas_call x0 -> x1, Pallas kernels: none -> 36.9 us  [per_device(): pl.pallas_call(hand_over, out_shape=(full, full), in_specs=[hbm, hbm], ou...]
    unnamed x12 -> x0, local copies, waits for them, and re-layouts: 6.1 us -> none
    pallas_call x1, Pallas kernels: 47.7 us -> 49.5 us  [per_device(): pl.pallas_call(functools.partial(kernel, n_xd, n_ta), out_shape=(full, fu...]
where the time goes in v3:
time: 87.2 us; the launch traced here: 87 us
  Pallas kernels  86.4 us (99%)
    pallas_call x1, Pallas kernels, per_device(): pl.pallas_call(functools.partial(kernel, n_xd, n_ta), out_shape=(full, fu...  49.5 us
    pallas_call x1, Pallas kernels, per_device(): pl.pallas_call(hand_over, out_shape=(full, full), in_specs=[hbm, hbm], ou...  36.9 us

profile of v3, /device:TPU:0, one launch (start us, length us, event | category | flops | bytes accessed | tf_op | source)
XLA Modules:
  0.0 87.0 jit_solution(6028603244203210750)
XLA Ops:
  0.6 49.5 %shard_map.68 = (f32[4,2,3,3,16,128]{5,4,3,2,1,0:T(8,128)}, f32[4,2,3,3,16,128]{5,4,3,2,1,0:T(8,128)}) custom-call(f32[4,2,3,3,16,128]{5,4,3,2,1,0:T(8,128)} %bitcast.10, f32[4,2,3,3,16,128]{5,4,3,2,1,0:T(8,128)} %bitcast.11, f32[2,3,4,4096]{3,2,1,0:T(4,128)} %bitcast.12, s32[16,128]{1,0:T(8,128)} %bitcast.13, s32[4]{0:T(128)} %partner.1), custom_call_target="tpu_custom_call" | custom-call | tf_op jit(solution)/shard_map/pallas_call | solution.py:469
  50.1 36.9 %shard_map.69 = (f32[4,2,3,3,16,128]{5,4,3,2,1,0:T(8,128)}, f32[4,2,3,3,16,128]{5,4,3,2,1,0:T(8,128)}) custom-call(f32[4,2,3,3,16,128]{5,4,3,2,1,0:T(8,128)} %get-tuple-element.6.links, f32[4,2,3,3,16,128]{5,4,3,2,1,0:T(8,128)} %get-tuple-element.7.momenta), custom_call_target="tpu_custom_call" | custom-call | tf_op jit(solution)/shard_map/pallas_call | solution.py:510

commit v4 on v3

--- a/solution.py
+++ b/solution.py
@@ -22,26 +22,40 @@
 )
 
 
-def gather_noise(table, index, out):
+def gather_noise(table, index, out, entry, split, gathered):
     rows, lanes = index.shape
-    entries = table.shape[-1]
-    lane = jnp.bitwise_and(index[...], lanes - 1)
-    chunk = lax.div(index[...], lanes)
-
-    def one(k, carry):
-        part, colour = lax.div(k, 3), lax.rem(k, 3)
-        for spin in range(4):
-            total = jnp.zeros((rows, lanes), F32)
-            for c in range(entries // lanes):
-                row = table[part, colour, spin : spin + 1, c * lanes : (c + 1) * lanes]
-                value = jnp.take_along_axis(
-                    jnp.broadcast_to(row, (rows, lanes)), lane, axis=1, mode="promise_in_bounds"
-                )
+    chunks = table.shape[-1] // lanes
+    for c in range(chunks):
+        for part in range(2):
+            for colour in range(3):
+                at = c * 24 + part * 12 + colour * 4
+                entry[at : at + 4] = table[part, colour, :, c * lanes : (c + 1) * lanes]
+    rest = entry[...]
+    for n in range(3):
+        piece = rest.astype(jnp.bfloat16)
+        split[:, n * lanes : (n + 1) * lanes] = piece
+        rest = rest - piece.astype(F32)
+    lane = lax.broadcasted_iota(jnp.int32, (lanes, lanes), 0)
+    for r in range(0, rows, 2):
+        hot = []
+        for j in range(2):
+            wanted = jnp.bitwise_and(index[r + j : r + j + 1], lanes - 1)
+            hot.append(jnp.where(lane == wanted, 1.0, 0.0).astype(jnp.bfloat16))
+        pair = jnp.concatenate(hot, axis=1)
+        picked = jnp.dot(
+            split[...], jnp.concatenate([pair] * 3, axis=0), preferred_element_type=F32
+        )
+        for j in range(2):
+            chunk = jnp.broadcast_to(lax.div(index[r + j : r + j + 1], lanes), (24, lanes))
+            total = picked[0:24, j * lanes : (j + 1) * lanes]
+            for c in range(1, chunks):
+                value = picked[c * 24 : (c + 1) * 24, j * lanes : (j + 1) * lanes]
                 total = jnp.where(chunk == c, value, total)
-            out[part, spin, colour] = total
-        return carry
-
-    lax.fori_loop(0, 6, one, 0)
+            gathered[:, r + j] = total
+    for part in range(2):
+        for colour in range(3):
+            for spin in range(4):
+                out[part, spin, colour] = gathered[part * 12 + colour * 4 + spin]
 
 
 def times_i(re, im, g_re, g_im):
@@ -154,7 +168,7 @@
 
 def kernel(
     n_xd, n_ta, u_hbm, m_hbm, table_hbm, index_hbm, partner, u_final, m_final,
-    u_in, m_in, table, index, u_out, m_out, noise,
+    u_in, m_in, table, index, u_out, m_out, noise, entry, split, gathered,
     h0, q0, h2, q2, phi, resp, acc, ahead, moved, f_perm, mom,
     face_out, face_in, time_out, time_in, force_out, force_in,
     face_s, face_r, time_s, time_r, force_s, force_r, load_s, store_s,
@@ -184,7 +198,7 @@
         pl.semaphore_signal(barrier, inc=1, device_id=other, device_id_type=MESH)
     loads[3].wait()
     loads[2].wait()
-    gather_noise(table, index, noise)
+    gather_noise(table, index, noise, entry, split, gathered)
     pl.semaphore_wait(barrier, 5)
     loads[0].wait()
 
@@ -442,15 +456,20 @@
         copy.wait()
 
 
-def hand_over(links, momenta, links_out, momenta_out, sems):
-    copies = [
-        pltpu.make_async_copy(source.at[mu], out.at[mu], sems.at[n, mu])
-        for mu in range(4)
-        for n, (source, out) in enumerate(((links, links_out), (momenta, momenta_out)))
-    ]
-    for copy in copies:
+def hand_over(links, momenta, links_out, momenta_out, stage, in_s, out_s):
+    pairs = ((links, links_out), (momenta, momenta_out))
+    taken, given = [], []
+    for n, (source, out) in enumerate(pairs):
+        for mu in range(4):
+            slot = stage.at[n, mu]
+            taken.append(pltpu.make_async_copy(source.at[mu], slot, in_s.at[n, mu]))
+            given.append(pltpu.make_async_copy(slot, out.at[mu], out_s.at[n, mu]))
+    for copy in taken:
         copy.start()
-    for copy in copies:
+    for arrived, leaving in zip(taken, given):
+        arrived.wait()
+        leaving.start()
+    for copy in given:
         copy.wait()
 
 
@@ -461,6 +480,7 @@
     n_xd, n_ta = lax.axis_size("xd"), lax.axis_size("ta")
     hbm = pl.BlockSpec(memory_space=pltpu.HBM)
     half = (2, 2, 3)
+    chunks = noise_table.shape[-1] // n3
     faces = 8 + 2 * MD_STEPS + 2 * (MD_STEPS - 1)
     times = 4 + MD_STEPS + (MD_STEPS - 1)
     field = (2, 4, 3, rows, n3)
@@ -479,6 +499,9 @@
             pltpu.VMEM(lead + (rows, n3), F32),
             pltpu.VMEM(lead + (rows, n3), F32),
             pltpu.VMEM(field, F32),
+            pltpu.VMEM((24 * chunks, n3), F32),
+            pltpu.VMEM((24 * chunks, 3 * n3), jnp.bfloat16),
+            pltpu.VMEM((24, rows, n3), F32),
             pltpu.VMEM(half + (rows + 8, n3), F32),
             pltpu.VMEM(half + (rows + 8, n3), F32),
             pltpu.VMEM(half + (rows + 8, n3), F32),
@@ -512,7 +535,7 @@
         out_shape=(full, full),
         in_specs=[hbm, hbm],
         out_specs=(hbm, hbm),
-        scratch_shapes=[dma((2, 4))],
+        scratch_shapes=[pltpu.VMEM((2,) + lead + (rows, n3), F32), dma((2, 4)), dma((2, 4))],
     )(new_links, new_momenta)
     return new_links.reshape(gauge_links.shape), new_momenta.reshape(momenta.shape)
 

time: 87.2 us -> 52.2 us (0.60)
  Pallas kernels: 86.4 us -> 51.3 us
    pallas_call x1, Pallas kernels: 36.9 us -> 2.15 us  [per_device(): pl.pallas_call(hand_over, out_shape=(full, full), in_specs=[hbm, hbm], ou...]
where the time goes in v4:
time: 52.2 us; the launch traced here: 52 us
  Pallas kernels  51.3 us (98%)
  between operations  0.64 us (1%)
    pallas_call x1, Pallas kernels, per_device(): pl.pallas_call(functools.partial(kernel, n_xd, n_ta), out_shape=(full, fu...  49.2 us
    pallas_call x1, Pallas kernels, per_device(): pl.pallas_call(hand_over, out_shape=(full, full), in_specs=[hbm, hbm], ou...  2.15 us

profile of v4, /device:TPU:0, one launch (start us, length us, event | category | flops | bytes accessed | tf_op | source)
XLA Modules:
  0.0 52.0 jit_solution(17819629113207393146)
XLA Ops:
  0.6 49.2 %shard_map.68 = (f32[4,2,3,3,16,128]{5,4,3,2,1,0:T(8,128)}, f32[4,2,3,3,16,128]{5,4,3,2,1,0:T(8,128)}) custom-call(f32[4,2,3,3,16,128]{5,4,3,2,1,0:T(8,128)} %bitcast.10, f32[4,2,3,3,16,128]{5,4,3,2,1,0:T(8,128)} %bitcast.11, f32[2,3,4,4096]{3,2,1,0:T(4,128)} %bitcast.12, s32[16,128]{1,0:T(8,128)} %bitcast.13, s32[4]{0:T(128)} %partner.1), custom_call_target="tpu_custom_call" | custom-call | tf_op jit(solution)/shard_map/pallas_call | solution.py:489
  49.8 2.1 %shard_map.69 = (f32[4,2,3,3,16,128]{5,4,3,2,1,0:T(8,128)}, f32[4,2,3,3,16,128]{5,4,3,2,1,0:T(8,128)}) custom-call(f32[4,2,3,3,16,128]{5,4,3,2,1,0:T(8,128)} %get-tuple-element.6.links, f32[4,2,3,3,16,128]{5,4,3,2,1,0:T(8,128)} %get-tuple-element.7.momenta), custom_call_target="tpu_custom_call" | custom-call | tf_op jit(solution)/shard_map/pallas_call | solution.py:533
